TPU v7x, 128 devices: a whole 4x4x4 slice. The times are simulated.
128 devices in a mesh: frames: 32 (over z, x, core), rows: 4 (over y).
Axes of the slice: x: 4, y: 4, z: 4, core: 2. Of those that a mesh axis runs over, the one named last changes fastest.
Arguments:
- latents: bfloat16 [128, 32, 18, 1280], P('frames', 'rows')
- first_gain: float32 [1280], replicated, may hold values from 0.1 to 1.9
- first_shift: float32 [1280], replicated, may hold values from -3 to 3
- spatial_kernel: bfloat16 [3, 3, 1280, 1280], P(None, None, 'frames'), may hold values from -0.0546875 to 0.0546875
- spatial_bias: float32 [1280], replicated, may hold values from -2 to 2
- second_gain: float32 [1280], replicated, may hold values from 0.1 to 1.9
- second_shift: float32 [1280], replicated, may hold values from -3 to 3
- temporal_kernel: bfloat16 [3, 1280, 1280], replicated, may hold values from -0.09375 to 0.09375
- temporal_bias: float32 [1280], replicated, may hold values from -2 to 2
- frame_slot: int32 [100], replicated, may hold values from 0 to 127, as said below
Outputs:
- block_output: bfloat16 [128, 32, 18, 1280], P('frames', 'rows')
Inputs may be any that keep to these rules, and one draw needn't show every extreme that they name: `frame_slot`: the 100 entries are distinct; device i of frames holds slots i * 4 to (i + 1) * 4 - 1; in every draw all 4 slots of some device are used, and slots 0 and 127 are used.
All inputs are finite; a program needn't handle non-finite values.
Results may differ from a plain program's by a relative error of at most 0.0018.
The roundings to bfloat16 on the way count: a program that leaves them out, or rounds other values in their place, can miss the bound.
Values may be sent and summed in bfloat16 or wider, within the bound.
A program may use at most 320 MiB of HBM per device.

v0:
```python
import jax
import jax.numpy as jnp
from jax import lax
from jax.sharding import PartitionSpec as P

FRAMES = 25
GROUPS = 32


norm_epsilon = 1e-06


def extended_2(block, sides, width):
    for axis, dim in sides:
        count = lax.axis_size(axis)
        forward = [(i, i + 1) for i in range(count - 1)]
        backward = [(target, source) for source, target in forward]
        low = lax.ppermute(
            lax.slice_in_dim(block, block.shape[dim] - width, None, axis=dim), axis, forward
        )
        high = lax.ppermute(lax.slice_in_dim(block, 0, width, axis=dim), axis, backward)
        block = jnp.concatenate([low, block, high], axis=dim)
    return block


def add_taps(summed, kernel_piece, source, band_rows, columns):
    depth = kernel_piece.shape[2]
    for row_tap in range(3):
        for col_tap in range(3):
            window = source[
                :, row_tap : row_tap + band_rows, col_tap : col_tap + columns, :
            ].reshape(-1, depth)
            summed = summed + jnp.dot(
                window, kernel_piece[row_tap, col_tap], preferred_element_type=jnp.float32
            )
    return summed


def body(
    latents,
    first_gain,
    first_shift,
    spatial_kernel,
    spatial_bias,
    second_gain,
    second_shift,
    temporal_kernel,
    temporal_bias,
    frame_slot,
):
    slot_count, band_rows, columns, channels = latents.shape
    frame_devices = lax.axis_size("frames")
    row_devices = lax.axis_size("rows")
    group_width = channels // GROUPS
    band_cells = band_rows * columns
    frame_total = frame_slot.shape[0]
    videos = frame_total // FRAMES
    all_slots = slot_count * frame_devices
    pixel_slots = (band_cells + frame_devices - 1) // frame_devices
    inputs = latents.astype(jnp.float32).reshape(slot_count, band_cells, GROUPS, group_width)
    band_sum = jnp.sum(inputs, axis=(1, 3))
    band_square = jnp.sum(inputs * inputs, axis=(1, 3))
    frame_sum, frame_square = lax.psum((band_sum, band_square), "rows")
    entries = band_cells * row_devices * group_width
    average = (frame_sum / entries)[:, None, :, None]
    squares = (frame_square / entries)[:, None, :, None]
    scaled = (inputs - average) * lax.rsqrt(squares - average * average + norm_epsilon)
    hidden_one = jax.nn.silu(scaled.reshape(latents.shape) * first_gain + first_shift).astype(
        jnp.bfloat16
    )
    extended = extended_2(hidden_one, (("rows", 1),), 1)
    padded = jnp.pad(extended, ((0, 0), (0, 0), (1, 1), (0, 0)))
    empty = jnp.zeros((slot_count * band_cells, channels), jnp.float32)
    whole_kernel = lax.all_gather(spatial_kernel, "frames", axis=2, tiled=True)
    summed = add_taps(empty, whole_kernel, padded, band_rows, columns)
    spatial = (latents.astype(jnp.float32) + summed.reshape(latents.shape) + spatial_bias).astype(
        jnp.bfloat16
    )
    flat = spatial.reshape(slot_count, band_cells, channels)
    flat = jnp.pad(flat, ((0, 0), (0, frame_devices * pixel_slots - band_cells), (0, 0)))
    outgoing = flat.reshape(slot_count, frame_devices, pixel_slots, channels)
    arrived = lax.all_to_all(outgoing, "frames", split_axis=1, concat_axis=0, tiled=True).reshape(
        all_slots, pixel_slots, channels
    )
    ordered = arrived[frame_slot].reshape(videos, FRAMES, pixel_slots, channels)
    ordered_values = ordered.astype(jnp.float32)
    grouped = ordered_values.reshape(videos, FRAMES * pixel_slots, GROUPS, group_width)
    clip_sum, clip_square = lax.psum(
        (jnp.sum(grouped, axis=(1, 3)), jnp.sum(grouped * grouped, axis=(1, 3))), ("frames", "rows")
    )
    clip_entries = FRAMES * band_cells * row_devices * group_width
    clip_average = (clip_sum / clip_entries)[:, None, :, None]
    clip_squares = (clip_square / clip_entries)[:, None, :, None]
    clip_scaled = (grouped - clip_average) * lax.rsqrt(
        clip_squares - clip_average * clip_average + norm_epsilon
    )
    hidden_two = jax.nn.silu(
        clip_scaled.reshape(ordered.shape) * second_gain + second_shift
    ).astype(jnp.bfloat16)
    extended_two = jnp.pad(hidden_two, ((0, 0), (1, 1), (0, 0), (0, 0)))
    temporal = jnp.zeros((videos * FRAMES * pixel_slots, channels), jnp.float32)
    for frame_tap in range(3):
        window = extended_two[:, frame_tap : frame_tap + FRAMES].reshape(-1, channels)
        temporal = temporal + jnp.dot(
            window, temporal_kernel[frame_tap], preferred_element_type=jnp.float32
        )
    mixed = (ordered_values + temporal.reshape(ordered.shape) + temporal_bias).astype(jnp.bfloat16)
    placed = jnp.zeros((all_slots, pixel_slots, channels), jnp.bfloat16)
    placed = placed.at[frame_slot].set(mixed.reshape(frame_total, pixel_slots, channels))
    returned = lax.all_to_all(
        placed.reshape(frame_devices, slot_count, pixel_slots, channels),
        "frames",
        split_axis=0,
        concat_axis=2,
        tiled=True,
    )
    result = returned.reshape(slot_count, frame_devices * pixel_slots, channels)[:, :band_cells]
    return result.reshape(latents.shape)


def solution(mesh):
    in_specs = (
        P("frames", "rows", None, None),
        P(),
        P(),
        P(None, None, "frames", None),
        P(),
        P(),
        P(),
        P(),
        P(),
        P(),
    )
    out_specs = P("frames", "rows", None, None)
    return jax.shard_map(body, mesh=mesh, in_specs=in_specs, out_specs=out_specs, check_vma=False)
```

profile of v0, /device:TPU:1, one launch (start us, length us, event | category | flops | bytes accessed | tf_op | source)
XLA Modules:
  0.0 382.0 jit_solution(14281342457052833030)
XLA Ops:
  6.5 0.7 all-gather.2.cloned.1.call-update
  7.3 2.1 convert_reduce_fusion
  9.8 9.6 %all-reduce.4 = (f32[4,32]{1,0:T(4,128)S(1)}, f32[4,32]{1,0:T(4,128)S(1)}) all-reduce(f32[4,32]{1,0:T(4,128)S(1)} %reduce_sum.54, f32[4,32]{1,0:T(4,128)S(1)} %reduce_sum.51), channel_id=1, replica_groups=mesh['frames'=32,'rows'=4] {'rows'}, use_global_device_ids=true, to_apply=%region_5.6 | all-reduce | flops 256 | bytes 2048 | tf_op jit(solution)/shard_map/psum | solution.py:63
  19.7 1.4 fusion.9
  21.2 0.8 fusion.32
  22.0 2.0 collective-permute-start
  23.9 1.3 collective-permute-start.1
  25.2 1.4 reshape.153
  26.7 4.8 %collective-permute-done.1 = bf16[4,1,18,1280]{3,2,1,0:T(8,128)(2,1)} collective-permute-done((bf16[4,1,18,1280]{3,2,1,0:T(8,128)(2,1)}, bf16[4,1,18,1280]{3,2,1,0:T(8,128)(2,1)}, u32[]{:S(2)}, u32[]{:S(2)}) %collective-permute-start.1) | collective-permute-done | bytes 184352 | tf_op jit(solution)/shard_map/ppermute | solution.py:21
  31.5 2.1 fusion.30
  33.6 4.7 %fusion.31 = (bf16[4,8,18,1280]{3,2,1,0:T(8,128)(2,1)}, bf16[4,8,18,1280]{3,2,1,0:T(8,128)(2,1)}, bf16[4,8,18,1280]{3,2,1,0:T(8,128)(2,1)}, bf16[4,8,18,1280]{3,...) fusion(bf16[4,10,20,1280]{3,2,1,0:T(8,128)(2,1)S(1)} %fusion.30), kind=kLoop, calls=%fused_computation.72 | loop fusion | bytes 17694720 | tf_op jit(solution)/shard_map/slice | solution.py:30
  38.2 3.6 reshape.149
  41.8 3.2 pad_maximum_fusion
  45.0 3.7 reshape.150
  48.7 3.6 reshape.151
  52.3 1.4 reshape.152
  53.7 3.7 reshape.154
  57.4 3.6 reshape.155
  60.9 1.3 reshape.157
  62.3 2.7 reshape.156
  64.9 51.8 %all-gather.2.cloned.1.call-done = bf16[3,3,1280,1280]{3,2,1,0:T(8,128)(2,1)} async-done(((bf16[3,3,40,1280]{3,2,1,0:T(8,128)(2,1)}), bf16[3,3,1280,1280]{3,2,1,0:T(8,128)(2,1)}) %all-gather.2.cloned.1.call-update) | async-done | bytes 29491216 | tf_op jit(solution)/shard_map/all_gather | solution.py:74
  116.7 6.2 %fusion.15 = f32[576,1280]{1,0:T(8,128)} fusion(bf16[576,1280]{1,0:T(8,128)(2,1)} %reshape.149, bf16[3,3,1280,1280]{3,2,1,0:T(8,128)(2,1)} %all-gather.2.cloned.1.call-done), kind=kOutput, calls=%fused_computation.43 | convolution fusion | flops 1887436800 | bytes 7700480 | tf_op jit(solution)/shard_map/dot_general | solution.py:33
  122.9 4.2 %fusion.14 = f32[576,1280]{1,0:T(8,128)S(1)} fusion(bf16[576,1280]{1,0:T(8,128)(2,1)S(1)} %copy-done.9, bf16[3,3,1280,1280]{3,2,1,0:T(8,128)(2,1)} %all-gather.2.cloned.1.call-done), kind=kOutput, calls=%fused_computation.34 | convolution fusion | flops 1887436800 | bytes 7700480 | tf_op jit(solution)/shard_map/dot_general | solution.py:33
  127.1 7.3 %convolution_add_fusion.6 = f32[576,1280]{1,0:T(8,128)} fusion(f32[576,1280]{1,0:T(8,128)} %fusion.15, bf16[576,1280]{1,0:T(8,128)(2,1)S(1)} %copy-done.8, bf16[3,3,1280,1280]{3,2,1,0:T(8,128)(2,1)} %all-gather.2.cloned.1.call-done), kind=kOutput, calls=%fused_computation.29 | convolution fusion | flops 1888174080 | bytes 10649600 | tf_op jit(solution)/shard_map/dot_general | solution.py:33
  134.4 2.2 copy-done.18
  136.6 0.6 copy-done.7
  137.2 5.6 %convolution_add_fusion.5 = f32[576,1280]{1,0:T(8,128)} fusion(f32[576,1280]{1,0:T(8,128)} %convolution_add_fusion.6, bf16[576,1280]{1,0:T(8,128)(2,1)S(1)} %copy-done.7, bf16[3,3,1280,1280]{3,2,1,0:T(8,128)(2,1)S(1)} %copy-done.18), kind=kOutput, calls=%fused_computation.28 | convolution fusion | flops 1888174080 | bytes 10649600 | tf_op jit(solution)/shard_map/dot_general | solution.py:33
  142.9 5.6 %convolution_add_fusion.4 = f32[576,1280]{1,0:T(8,128)} fusion(f32[576,1280]{1,0:T(8,128)} %convolution_add_fusion.5, bf16[576,1280]{1,0:T(8,128)(2,1)S(1)} %copy-done.6, bf16[3,3,1280,1280]{3,2,1,0:T(8,128)(2,1)S(1)} %copy-done.18), kind=kOutput, calls=%fused_computation.27 | convolution fusion | flops 1888174080 | bytes 10649600 | tf_op jit(solution)/shard_map/dot_general | solution.py:33
  148.5 5.6 %convolution_add_fusion.3 = f32[576,1280]{1,0:T(8,128)} fusion(f32[576,1280]{1,0:T(8,128)} %convolution_add_fusion.4, bf16[576,1280]{1,0:T(8,128)(2,1)S(1)} %copy-done.3, bf16[3,3,1280,1280]{3,2,1,0:T(8,128)(2,1)S(1)} %copy-done.18), kind=kOutput, calls=%fused_computation.26 | convolution fusion | flops 1888174080 | bytes 10649600 | tf_op jit(solution)/shard_map/dot_general | solution.py:33
  154.2 5.6 %convolution_add_fusion.2 = f32[576,1280]{1,0:T(8,128)} fusion(f32[576,1280]{1,0:T(8,128)} %convolution_add_fusion.3, bf16[576,1280]{1,0:T(8,128)(2,1)S(1)} %copy-done.5, bf16[3,3,1280,1280]{3,2,1,0:T(8,128)(2,1)S(1)} %copy-done.18), kind=kOutput, calls=%fused_computation.25 | convolution fusion | flops 1888174080 | bytes 10649600 | tf_op jit(solution)/shard_map/dot_general | solution.py:33
  159.8 5.7 %convolution_add_fusion.1 = f32[576,1280]{1,0:T(8,128)} fusion(f32[576,1280]{1,0:T(8,128)} %convolution_add_fusion.2, bf16[576,1280]{1,0:T(8,128)(2,1)S(1)} %copy-done.4, bf16[3,3,1280,1280]{3,2,1,0:T(8,128)(2,1)S(1)} %copy-done.18), kind=kOutput, calls=%fused_computation.24 | convolution fusion | flops 1888174080 | bytes 10649600 | tf_op jit(solution)/shard_map/dot_general | solution.py:33
  165.6 5.7 %fusion.13 = f32[576,1280]{1,0:T(8,128)} fusion(f32[576,1280]{1,0:T(8,128)S(1)} %fusion.14, f32[576,1280]{1,0:T(8,128)} %convolution_add_fusion.1, bf16[576,1280]{1,0:T(8,128)(2,1)S(1)} %reshape.156, bf16[3,3,1280,1280]{3,2,1,0:T(8,128)(2,1)S(1)} %copy-done.18), kind=kOutput, calls=%fused_computation.30 | convolution fusion | flops 1888911360 | bytes 13598720 | tf_op jit(solution)/shard_map/dot_general | solution.py:33
  171.2 4.2 %reshape.158 = f32[4,8,18,1280]{3,2,1,0:T(8,128)} reshape(f32[576,1280]{1,0:T(8,128)} %fusion.13) | data formatting | bytes 5898240 | tf_op jit(solution)/shard_map/reshape | solution.py:76
  175.4 2.6 fusion.12
  178.0 1.1 copy.41
  179.2 1.8 pad.13
  181.0 5.2 %all-to-all-start = ((bf16[4,32,5,1280]{3,0,2,1:T(4,128)(2,1)}), bf16[4,32,5,1280]{3,0,2,1:T(4,128)(2,1)S(1)}, u32[]{:S(2)}, u32[]{:S(2)}) async-start(bf16[4,32,5,1280]{3,0,2,1:T(4,128)(2,1)} %bitcast.10), calls=%async_computation | async-start | bytes 3276800 | tf_op jit(solution)/shard_map/all_to_all | solution.py:82
  186.3 22.7 %all-to-all-done = bf16[4,32,5,1280]{3,0,2,1:T(4,128)(2,1)S(1)} async-done(((bf16[4,32,5,1280]{3,0,2,1:T(4,128)(2,1)}), bf16[4,32,5,1280]{3,0,2,1:T(4,128)(2,1)S(1)}, u32[]{:S(2)}, u32[]{:S(2)}) %all-to-all-start) | async-done | bytes 1638432 | tf_op jit(solution)/shard_map/all_to_all | solution.py:82
  209.0 2.0 copy.51
  211.0 2.5 gather_fusion
  213.5 2.5 convert_reduce_fusion.1
  216.0 2.5 reduce_sum.59
  218.5 1.7 reduce_sum.72
  220.1 2.5 reduce_sum.74
  222.6 1.7 reduce_sum.75
  224.3 65.3 %all-reduce.3 = (f32[4,32]{1,0:T(4,128)S(1)}, f32[4,32]{1,0:T(4,128)S(1)}) all-reduce(f32[4,32]{1,0:T(4,128)S(1)} %reduce_sum.75, f32[4,32]{1,0:T(4,128)S(1)} %reduce_sum.72), channel_id=1, replica_groups=mesh['frames'=32,'rows'=4] {'frames','rows'}, use_global_device_ids=true, to_apply=%region_11.12 | all-reduce | flops 256 | bytes 2048 | tf_op jit(solution)/shard_map/psum | solution.py:88
  290.7 1.3 multiply_convert_fusion
  292.0 2.2 pad_slice_fusion
  294.1 2.1 copy.46
  296.2 2.0 copy.45
  298.3 2.6 reshape.162
  300.9 3.6 convert_element_type.61
  304.5 3.5 copy.47
  308.0 3.6 reshape.163
  311.6 3.9 %fusion.18 = f32[500,1280]{1,0:T(8,128)S(1)} fusion(bf16[500,1280]{1,0:T(8,128)(2,1)S(1)} %reshape.162, bf16[3,1280,1280]{2,1,0:T(8,128)(2,1)} %param.17), kind=kOutput, calls=%fused_computation.46 | convolution fusion | flops 1638400000 | bytes 7116800 | tf_op jit(solution)/shard_map/dot_general | solution.py:104
  315.5 3.9 %convolution_add_fusion.8 = f32[500,1280]{1,0:T(8,128)S(1)} fusion(f32[500,1280]{1,0:T(8,128)S(1)} %fusion.18, bf16[500,1280]{1,0:T(8,128)(2,1)S(1)} %copy-done.10, bf16[3,1280,1280]{2,1,0:T(8,128)(2,1)} %param.17), kind=kOutput, calls=%fused_computation.32 | convolution fusion | flops 1639040000 | bytes 9676800 | tf_op jit(solution)/shard_map/dot_general | solution.py:104
  319.5 5.3 %convolution_add_fusion.7 = f32[500,1280]{1,0:T(8,128)} fusion(f32[500,1280]{1,0:T(8,128)S(1)} %convolution_add_fusion.8, bf16[500,1280]{1,0:T(8,128)(2,1)S(1)} %copy-done.11, bf16[3,1280,1280]{2,1,0:T(8,128)(2,1)} %param.17), kind=kOutput, calls=%fused_computation.31 | convolution fusion | flops 1639040000 | bytes 9676800 | tf_op jit(solution)/shard_map/dot_general | solution.py:104
  324.7 4.5 %reshape.164 = f32[100,5,1280]{2,1,0:T(8,128)} reshape(f32[500,1280]{1,0:T(8,128)} %convolution_add_fusion.7) | data formatting | bytes 5120000 | tf_op jit(solution)/shard_map/reshape | solution.py:107
  329.2 4.0 %add_convert_fusion = bf16[100,5,1280]{2,1,0:T(8,128)(2,1)} fusion(f32[100,5,1280]{2,1,0:T(8,128)} %reshape.164, bf16[100,5,1280]{2,1,0:T(8,128)(2,1)S(1)} %gather_fusion, f32[1280]{0:T(1024)S(1)} %copy-done.16), kind=kLoop, calls=%fused_computation.9 | loop fusion | flops 2560000 | bytes 5125120 | tf_op jit(solution)/shard_map/convert_element_type | solution.py:107
  333.4 10.6 %scatter_fusion = bf16[128,5,1280]{2,1,0:T(8,128)(2,1)S(1)} fusion(bf16[128,5,1280]{2,1,0:T(8,128)(2,1)S(1)} %broadcast_in_dim.4, s32[100]{0:T(128)S(1)} %compare_select_fusion, bf16[100,5,1280]{2,1,0:T(8,128)(2,1)} %add_convert_fusion), kind=kCustom, calls=%fused_computation.1 | custom fusion | bytes 3840400 | tf_op jit(solution)/shard_map/scatter | solution.py:109
  344.0 0.7 copy.49
  344.7 28.4 %all_to_all.30 = bf16[32,4,5,1280]{3,1,2,0:T(4,128)(2,1)S(1)} all-to-all(bf16[32,4,5,1280]{3,1,2,0:T(4,128)(2,1)S(1)} %copy.49), channel_id=1, replica_groups=mesh['frames'=32,'rows'=4] {'frames'}, dimensions={0} | all-to-all | bytes 3276800 | tf_op jit(solution)/shard_map/all_to_all | solution.py:110
  373.1 0.5 slice.126
  373.6 1.4 copy.50
  (58 shorter events, 2.2 us)
Async XLA Ops:
  6.5 13.2 %copy-start = (bf16[4,8,18,1280]{3,1,2,0:T(8,128)(2,1)S(1)}, bf16[4,8,18,1280]{3,1,2,0:T(8,128)(2,1)}, u32[]{:S(2)}) copy-start(bf16[4,8,18,1280]{3,1,2,0:T(8,128)(2,1)} %param.10) | copy-start | bytes 4423684
  6.5 13.2 %copy-start.13 = (f32[1280]{0:T(1024)S(1)}, f32[1280]{0:T(1024)}, u32[]{:S(2)}) copy-start(f32[1280]{0:T(1024)} %param.11) | copy-start | bytes 15364
  6.5 13.2 %copy-start.12 = (f32[1280]{0:T(1024)S(1)}, f32[1280]{0:T(1024)}, u32[]{:S(2)}) copy-start(f32[1280]{0:T(1024)} %param.12) | copy-start | bytes 15364
  6.5 110.2 %all-gather.2.cloned.1.call-start = ((), (), s32[]{:S(2)}) async-start(), calls=%async_computation.2 | async-start | bytes 30412800 | tf_op jit(solution)/shard_map/all_gather | solution.py:74
  22.0 4.7 %collective-permute-start = (bf16[4,1,18,1280]{3,2,1,0:T(8,128)(2,1)}, bf16[4,1,18,1280]{3,2,1,0:T(8,128)(2,1)}, u32[]{:S(2)}, u32[]{:S(2)}) collective-permute-start(bf16[4,1,18,1280]{3,2,1,0:T(8,128)(2,1)} %get-tuple-element.21), channel_id=1, source_target_pairs={{0,1},{1,2},{2,3},{4,5},{5,6},{6,7},{8,9},{9,10},{10,11},{12,13},{... | collective-permute-start | bytes 552968 | tf_op jit(solution)/shard_map/ppermute | solution.py:18
  23.9 7.5 %collective-permute-start.1 = (bf16[4,1,18,1280]{3,2,1,0:T(8,128)(2,1)}, bf16[4,1,18,1280]{3,2,1,0:T(8,128)(2,1)}, u32[]{:S(2)}, u32[]{:S(2)}) collective-permute-start(bf16[4,1,18,1280]{3,2,1,0:T(8,128)(2,1)} %get-tuple-element.22), channel_id=1, source_target_pairs={{1,0},{2,1},{3,2},{5,4},{6,5},{7,6},{9,8},{10,9},{11,10},{13,12},{... | collective-permute-start | bytes 552968 | tf_op jit(solution)/shard_map/ppermute | solution.py:21
  45.0 7.3 %copy-start.2 = (bf16[4,8,18,1280]{3,2,1,0:T(8,128)(2,1)S(1)}, bf16[4,8,18,1280]{3,2,1,0:T(8,128)(2,1)}, u32[]{:S(2)}) copy-start(bf16[4,8,18,1280]{3,2,1,0:T(8,128)(2,1)} %get-tuple-element.15) | copy-start | bytes 4423684
  53.7 7.3 %copy-start.1 = (bf16[4,8,18,1280]{3,2,1,0:T(8,128)(2,1)S(1)}, bf16[4,8,18,1280]{3,2,1,0:T(8,128)(2,1)}, u32[]{:S(2)}) copy-start(bf16[4,8,18,1280]{3,2,1,0:T(8,128)(2,1)} %get-tuple-element.18) | copy-start | bytes 4423684
  116.7 6.2 %copy-start.9 = (bf16[576,1280]{1,0:T(8,128)(2,1)S(1)}, bf16[576,1280]{1,0:T(8,128)(2,1)}, u32[]{:S(2)}) copy-start(bf16[576,1280]{1,0:T(8,128)(2,1)} %reshape.157) | copy-start | bytes 4423684
  122.9 4.2 %copy-start.8 = (bf16[576,1280]{1,0:T(8,128)(2,1)S(1)}, bf16[576,1280]{1,0:T(8,128)(2,1)}, u32[]{:S(2)}) copy-start(bf16[576,1280]{1,0:T(8,128)(2,1)} %reshape.150) | copy-start | bytes 4423684
  122.9 13.7 %copy-start.18 = (bf16[3,3,1280,1280]{3,2,1,0:T(8,128)(2,1)S(1)}, bf16[3,3,1280,1280]{3,2,1,0:T(8,128)(2,1)}, u32[]{:S(2)}) copy-start(bf16[3,3,1280,1280]{3,2,1,0:T(8,128)(2,1)} %all-gather.2.cloned.1.call-done) | copy-start | bytes 88473600
  127.1 10.2 %copy-start.7 = (bf16[576,1280]{1,0:T(8,128)(2,1)S(1)}, bf16[576,1280]{1,0:T(8,128)(2,1)}, u32[]{:S(2)}) copy-start(bf16[576,1280]{1,0:T(8,128)(2,1)} %reshape.151) | copy-start | bytes 4423684
  137.2 5.6 %copy-start.6 = (bf16[576,1280]{1,0:T(8,128)(2,1)S(1)}, bf16[576,1280]{1,0:T(8,128)(2,1)}, u32[]{:S(2)}) copy-start(bf16[576,1280]{1,0:T(8,128)(2,1)} %reshape.152) | copy-start | bytes 4423684
  142.9 5.6 %copy-start.3 = (bf16[576,1280]{1,0:T(8,128)(2,1)S(1)}, bf16[576,1280]{1,0:T(8,128)(2,1)}, u32[]{:S(2)}) copy-start(bf16[576,1280]{1,0:T(8,128)(2,1)} %reshape.153) | copy-start | bytes 4423684
  148.5 5.6 %copy-start.5 = (bf16[576,1280]{1,0:T(8,128)(2,1)S(1)}, bf16[576,1280]{1,0:T(8,128)(2,1)}, u32[]{:S(2)}) copy-start(bf16[576,1280]{1,0:T(8,128)(2,1)} %reshape.154) | copy-start | bytes 4423684
  154.2 5.6 %copy-start.4 = (bf16[576,1280]{1,0:T(8,128)(2,1)S(1)}, bf16[576,1280]{1,0:T(8,128)(2,1)}, u32[]{:S(2)}) copy-start(bf16[576,1280]{1,0:T(8,128)(2,1)} %reshape.155) | copy-start | bytes 4423684
  171.2 4.2 %copy-start.17 = (f32[1280]{0:T(1024)S(1)}, f32[1280]{0:T(1024)}, u32[]{:S(2)}) copy-start(f32[1280]{0:T(1024)} %param.14) | copy-start | bytes 15364
  179.2 7.0 %copy-start.19 = (s32[100]{0:T(128)S(1)}, s32[100]{0:T(128)}, u32[]{:S(2)}) copy-start(s32[100]{0:T(128)} %param.19) | copy-start | bytes 1204
  181.0 28.0 %all-to-all-start = ((bf16[4,32,5,1280]{3,0,2,1:T(4,128)(2,1)}), bf16[4,32,5,1280]{3,0,2,1:T(4,128)(2,1)S(1)}, u32[]{:S(2)}, u32[]{:S(2)}) async-start(bf16[4,32,5,1280]{3,0,2,1:T(4,128)(2,1)} %bitcast.10), calls=%async_computation | async-start | bytes 3276800 | tf_op jit(solution)/shard_map/all_to_all | solution.py:82
  289.9 0.7 copy-start.14
  289.9 0.7 copy-start.15
  311.6 3.9 %copy-start.10 = (bf16[500,1280]{1,0:T(8,128)(2,1)S(1)}, bf16[500,1280]{1,0:T(8,128)(2,1)}, u32[]{:S(2)}) copy-start(bf16[500,1280]{1,0:T(8,128)(2,1)} %convert_element_type.61) | copy-start | bytes 3840004
  315.5 3.9 %copy-start.11 = (bf16[500,1280]{1,0:T(8,128)(2,1)S(1)}, bf16[500,1280]{1,0:T(8,128)(2,1)}, u32[]{:S(2)}) copy-start(bf16[500,1280]{1,0:T(8,128)(2,1)} %reshape.163) | copy-start | bytes 3840004
  324.7 4.5 %copy-start.16 = (f32[1280]{0:T(1024)S(1)}, f32[1280]{0:T(1024)}, u32[]{:S(2)}) copy-start(f32[1280]{0:T(1024)} %param.18) | copy-start | bytes 15364
Sparse Core Ops, SparseCore 0:
  9.7 106.9 all-gather.1
where the time goes:
time: 389 us; the launch traced here: 382 us
  blocking collectives  103 us (26%)
  local copies, waits for them, and re-layouts  88.6 us (23%)
  waiting for transfers between devices  80.1 us (21%)
  matrix products  64.6 us (17%)
  other arithmetic  23 us (6%)
  between operations  13.9 us (4%)
  starting transfers between devices  8.5 us (2%)
    psum x1, blocking collectives, body(): lax.psum((jnp.sum(grouped, axis=(1, 3)), jnp.sum(grouped * grouped, axis=...  65.3 us
    all_gather x1, waiting for transfers between devices, body(): whole_kernel = lax.all_gather(spatial_kernel, 'frames', axis=2, tiled=True)  51.8 us
    dot_general x9, matrix products, add_taps(): jnp.dot(window, kernel_piece[row_tap, col_tap], preferred_element_type=jn...  51.6 us
    all_to_all x1, blocking collectives, body(): lax.all_to_all(placed.reshape(frame_devices, slot_count, pixel_slots, cha...  28.4 us
    reshape x9, local copies, waits for them, and re-layouts, add_taps(): window = source[:, row_tap:row_tap + band_rows, col_tap:col_tap + columns...  24.9 us
    all_to_all x1, waiting for transfers between devices, body(): lax.all_to_all(outgoing, 'frames', split_axis=1, concat_axis=0, tiled=True)  22.7 us
    dot_general x3, matrix products, body(): jnp.dot(window, temporal_kernel[frame_tap], preferred_element_type=jnp.fl...  13 us
    scatter x1, local copies, waits for them, and re-layouts, body(): placed.at[frame_slot].set(mixed.reshape(frame_total, pixel_slots, channels))  10.6 us
  transfers between devices with their start and end apart: 4, of which 4 were waited for; matrix products, arithmetic and copies ran while one was open for 10% of the time, Pallas kernels for 0%

commit v1 on v0

v1 whole, which is shorter than its diff:
```python
import jax
import jax.numpy as jnp
from jax import lax
from jax.experimental import pallas as pl
from jax.experimental.pallas import tpu as pltpu
from jax.sharding import PartitionSpec as P

FRAMES = 25
GROUPS = 32
EPS = 1e-06
MESH = pl.DeviceIdType.MESH
C = 1280
LANES = 10
STAGES = 5
PITCH = 24
KINDS = 24


def group_indicator(tile):
    channel = lax.broadcasted_iota(jnp.int32, (128, 128), 0) + tile * 128
    first = lax.broadcasted_iota(jnp.int32, (128, 128), 1) * 40
    return jnp.where((channel >= first) & (channel < first + 40), 1.0, 0.0)


def group_indicator_t(tile):
    channel = lax.broadcasted_iota(jnp.int32, (128, 128), 1) + tile * 128
    first = lax.broadcasted_iota(jnp.int32, (128, 128), 0) * 40
    return jnp.where((channel >= first) & (channel < first + 40), 1.0, 0.0)


def exact_dot(a, b):
    return jnp.dot(a, b, preferred_element_type=jnp.float32, precision=lax.Precision.HIGHEST)


def spatial_kernel_body(
    lat,
    gain,
    shift,
    wk,
    bias,
    out,
    G,
    X,
    F,
    R,
    halo,
    RM,
    acc,
    pieces,
    stats,
    scales,
    send,
    recv,
    piece_send,
    piece_recv,
    piece_own,
    small_send,
    small_recv,
    lat_sem,
):
    fr = lax.axis_index("frames")
    y = lax.axis_index("rows")
    core = lax.rem(fr, 2)
    chip = lax.div(fr, 2)
    x = lax.rem(chip, 4)
    z = lax.div(chip, 4)
    u = x + core * (z - x)
    w = z + core * (x - z)
    par = lax.rem(y, 2)

    def wrap(v):
        return lax.rem(v + 4, 4)

    def same_core(u_, w_):
        return (((w_ + core * (u_ - w_)) * 4) + u_ + core * (w_ - u_)) * 2 + core

    u_up = {"frames": same_core(wrap(u + 1), w)}
    u_dn = {"frames": same_core(wrap(u - 1), w)}
    w_up = {"frames": same_core(u, wrap(w + 1))}
    w_dn = {"frames": same_core(u, wrap(w - 1))}
    sib = {"frames": fr + 1 - 2 * core}
    y_up = {"rows": wrap(y + 1)}
    y_dn = {"rows": wrap(y - 1)}
    y_op = {"rows": wrap(y + 2)}
    barrier = pltpu.get_barrier_semaphore()
    for peer in (u_up, u_dn, w_up, w_dn, sib, y_up, y_dn, y_op):
        pl.semaphore_signal(barrier, inc=1, device_id=peer, device_id_type=MESH)
    pl.semaphore_wait(barrier, 8)

    plane_tap = 3 * par

    def piece_copy(s):
        return pltpu.make_async_remote_copy(
            src_ref=wk.at[pl.ds(plane_tap, 6), :, pl.ds(pl.multiple_of(256 * s + 128 * (1 - core), 128), 128)],
            dst_ref=pieces.at[s, core],
            send_sem=piece_send.at[s],
            recv_sem=piece_recv.at[s],
            device_id=sib,
            device_id_type=MESH,
        )

    def piece_arrived(s):
        return pltpu.make_async_remote_copy(
            src_ref=pieces.at[s, 1 - core],
            dst_ref=pieces.at[s, 1 - core],
            send_sem=piece_send.at[s],
            recv_sem=piece_recv.at[s],
            device_id=sib,
            device_id_type=MESH,
        )

    def piece_local(s):
        return pltpu.make_async_copy(
            wk.at[pl.ds(plane_tap, 6), :, pl.ds(pl.multiple_of(256 * s + 128 * core, 128), 128)],
            pieces.at[s, core],
            piece_own.at[s],
        )

    for s in range(STAGES):
        piece_copy(s).start()
        piece_local(s).start()
    lat_copy = pltpu.make_async_copy(lat, R, lat_sem)
    lat_copy.start()

    def small(src, dst, k, target):
        return pltpu.make_async_remote_copy(
            src_ref=src,
            dst_ref=dst,
            send_sem=small_send.at[k],
            recv_sem=small_recv.at[k],
            device_id=target,
            device_id_type=MESH,
        )

    small(lat.at[:, 7], halo.at[0], 0, y_up).start()
    small(lat.at[:, 0], halo.at[1], 1, y_dn).start()

    def region(q, row, u0, count, tap, taps):
        return G.at[q, row, pl.ds(u0, count), pl.ds(tap, taps)]

    def mover(k, s, ref, target):
        return pltpu.make_async_remote_copy(
            src_ref=ref,
            dst_ref=ref,
            send_sem=send.at[s, k],
            recv_sem=recv.at[s, k],
            device_id=target,
            device_id_type=MESH,
        )

    rows = [w, wrap(w - 1), wrap(w + 1), wrap(w + 2)]
    sib_rows = [u, wrap(u - 1), wrap(u + 1), wrap(u + 2)]
    out_tap = 6 * par
    in_tap = 6 * (1 - par)
    pending = []

    def go(k, s, ref, target):
        copy = mover(k, s, ref, target)
        copy.start()
        pending.append(copy)

    def arrived(k, s, ref, source):
        mover(k, s, ref, source).wait_recv()

    def spread(i, s):
        q = 2 * s + core
        go(8 + 2 * i, s, region(q, rows[i], 0, 2, out_tap, 3), y_up)
        go(9 + 2 * i, s, region(q, rows[i], 2, 2, out_tap, 3), y_dn)
        go(16 + i, s, region(q, rows[i], 0, 4, plane_tap, 6), sib)

    def event0(s):
        piece_local(s).wait()
        piece_arrived(s).wait_recv()
        q = 2 * s + core

        def one(t, carry):
            both = jnp.concatenate(
                [pieces[s, 0, t].astype(jnp.float32), pieces[s, 1, t].astype(jnp.float32)], axis=0
            )
            G[q, w, u, plane_tap + t] = both.astype(jnp.bfloat16)
            return carry

        lax.fori_loop(0, 6, one, 0)
        unit = region(q, w, u, 1, plane_tap, 6)
        go(0, s, unit, u_up)
        go(1, s, unit, u_dn)

    def event1(s):
        q = 2 * s + core
        um, up = wrap(u - 1), wrap(u + 1)
        arrived(0, s, region(q, w, um, 1, plane_tap, 6), u_dn)
        go(2, s, region(q, w, um, 1, plane_tap, 3), u_up)
        arrived(1, s, region(q, w, up, 1, plane_tap, 6), u_up)
        go(3, s, region(q, w, up, 1, plane_tap + 3, 3), u_dn)

    def event2(s):
        q = 2 * s + core
        uo = wrap(u + 2)
        arrived(2, s, region(q, w, uo, 1, plane_tap, 3), u_dn)
        arrived(3, s, region(q, w, uo, 1, plane_tap + 3, 3), u_up)
        unit = region(q, w, 0, 4, plane_tap, 6)
        go(4, s, unit, w_up)
        go(5, s, unit, w_dn)
        spread(0, s)

    def event3(s):
        q = 2 * s + core
        arrived(4, s, region(q, rows[1], 0, 4, plane_tap, 6), w_dn)
        go(6, s, region(q, rows[1], 0, 2, plane_tap, 6), w_up)
        arrived(5, s, region(q, rows[2], 0, 4, plane_tap, 6), w_up)
        go(7, s, region(q, rows[2], 2, 2, plane_tap, 6), w_dn)
        spread(1, s)
        spread(2, s)

    def event4(s):
        q = 2 * s + core
        arrived(6, s, region(q, rows[3], 0, 2, plane_tap, 6), w_dn)
        arrived(7, s, region(q, rows[3], 2, 2, plane_tap, 6), w_up)
        spread(3, s)
        for i in range(3):
            from_y(i, s)

    def from_y(i, s):
        q = 2 * s + core
        arrived(8 + 2 * i, s, region(q, rows[i], 0, 2, in_tap, 3), y_dn)
        arrived(9 + 2 * i, s, region(q, rows[i], 2, 2, in_tap, 3), y_up)
        go(20 + i, s, region(q, rows[i], 0, 4, in_tap, 3), sib)

    def event5(s):
        from_y(3, s)
        q = 2 * s + 1 - core
        for i in range(4):
            arrived(16 + i, s, region(q, sib_rows[i], 0, 4, plane_tap, 6), sib)
            arrived(20 + i, s, region(q, sib_rows[i], 0, 4, in_tap, 3), sib)

    def conv(s):
        acc[...] = jnp.zeros_like(acc)

        def one(a, carry):
            for b in range(3):
                t = a * 3 + b
                even = G[2 * s, :, :, t].reshape(C, 128)
                odd = jnp.concatenate(
                    [G[2 * s + 1, i, j, t] for j in range(4) for i in range(4)], axis=0
                )
                kernel = jnp.concatenate([even, odd], axis=1)
                window = X[a, :, b * 16 : b * 16 + 288, :].reshape(576, C)
                acc[...] += jnp.dot(window, kernel, preferred_element_type=jnp.float32)
            return carry

        lax.fori_loop(0, 3, one, 0)
        cols = slice(256 * s, 256 * s + 256)
        base = RM[:, :, cols].reshape(576, 256).astype(jnp.float32)
        out[:, :, cols] = (
            (base + acc[...] + bias[:, cols]).astype(jnp.bfloat16).reshape(2, 288, 256)
        )

    def raw_rows():
        lat_copy.wait()

        def one(r, carry):
            for s in range(4):
                start = pl.multiple_of(((r + 1) * 4 + s) * PITCH, 8)
                for l in range(LANES):
                    F[l, pl.ds(start, 18), :] = R[s, r, :, l * 128 : l * 128 + 128].astype(
                        jnp.float32
                    )
            return carry

        lax.fori_loop(0, 8, one, 0)

        def sums(l, carry):
            total, square = [], []
            for s in range(4):
                a = jnp.zeros((18, 128), jnp.float32)
                b = jnp.zeros((18, 128), jnp.float32)
                for r in range(8):
                    v = F[l, ((r + 1) * 4 + s) * PITCH : ((r + 1) * 4 + s) * PITCH + 18, :]
                    a = a + v
                    b = b + v * v
                total.append(jnp.sum(a, axis=0, keepdims=True))
                square.append(jnp.sum(b, axis=0, keepdims=True))
            stats[y, l] = jnp.concatenate(total + square, axis=0)
            return carry

        lax.fori_loop(0, LANES, sums, 0)
        for k, peer in ((2, y_up), (3, y_dn), (4, y_op)):
            small(stats.at[y], stats.at[y], k, peer).start()

    def residual_rows():
        def one(c, carry):
            for l in range(LANES):
                for h in range(2):
                    v = F[l, pl.ds(4 * (4 * h + 1) * PITCH + c, 16, stride=PITCH), :]
                    RM[h, pl.ds(pl.multiple_of(c * 16, 16), 16), l * 128 : l * 128 + 128] = (
                        v.astype(jnp.bfloat16)
                    )
            return carry

        lax.fori_loop(0, 18, one, 0)

    def hidden_rows():
        small(lat.at[:, 7], halo.at[0], 0, y_up).wait_recv()
        small(lat.at[:, 0], halo.at[1], 1, y_dn).wait_recv()
        for side, r in ((0, 0), (1, 9)):
            for s in range(4):
                start = (r * 4 + s) * PITCH
                for l in range(LANES):
                    F[l, start : start + 18, :] = halo[
                        side, s, :, l * 128 : l * 128 + 128
                    ].astype(jnp.float32)
        small(stats.at[wrap(y - 1)], stats.at[wrap(y - 1)], 2, y_up).wait_recv()
        small(stats.at[wrap(y + 1)], stats.at[wrap(y + 1)], 3, y_dn).wait_recv()
        small(stats.at[wrap(y + 2)], stats.at[wrap(y + 2)], 4, y_op).wait_recv()
        grouped = jnp.zeros((8, 128), jnp.float32)
        for l in range(LANES):
            total = (stats[0, l] + stats[1, l]) + (stats[2, l] + stats[3, l])
            grouped = grouped + exact_dot(total, group_indicator(l))
        grouped = grouped * (1.0 / 23040.0)
        mean = grouped[0:4]
        rate = lax.rsqrt(grouped[4:8] - mean * mean + EPS)
        both = jnp.concatenate([rate, mean * rate], axis=0)
        for l in range(LANES):
            wide = exact_dot(both, group_indicator_t(l))
            g = gain[:, l * 128 : l * 128 + 128]
            b = shift[:, l * 128 : l * 128 + 128]
            scales[l] = jnp.concatenate([wide[0:4] * g, b - wide[4:8] * g], axis=0)

        def one(r, carry):
            inside = jnp.logical_and(
                jnp.logical_or(r > 0, y > 0), jnp.logical_or(r < 9, y < 3)
            )
            keep = jnp.where(inside, 1.0, 0.0)
            for s in range(4):
                start = pl.multiple_of((r * 4 + s) * PITCH, 8)
                for l in range(LANES):
                    v = F[l, pl.ds(start, PITCH), :] * scales[l, s : s + 1] + scales[
                        l, 4 + s : 5 + s
                    ]
                    v = v * (1.0 / (1.0 + jnp.exp(-v)))
                    F[l, pl.ds(start, PITCH), :] = jnp.where(keep > 0.5, v, 0.0)
            return carry

        lax.fori_loop(0, 10, one, 0)

    def window_rows():
        zero = jnp.zeros((16, C), jnp.bfloat16)
        for a in range(3):
            for h in range(2):
                X[a, h, 0:16, :] = zero
                X[a, h, 304:320, :] = zero

        def one(c, carry):
            for l in range(LANES):
                for h in range(2):
                    for a in range(3):
                        v = F[l, pl.ds(4 * (4 * h + a) * PITCH + c, 16, stride=PITCH), :]
                        X[
                            a,
                            h,
                            pl.ds(pl.multiple_of(c * 16 + 16, 16), 16),
                            l * 128 : l * 128 + 128,
                        ] = v.astype(jnp.bfloat16)
            return carry

        lax.fori_loop(0, 18, one, 0)

    for s in range(STAGES):
        event0(s)
    raw_rows()
    event1(0)
    event1(1)
    residual_rows()
    event2(0)
    event1(2)
    hidden_rows()
    event3(0)
    event2(1)
    event1(3)
    window_rows()
    event4(0)
    event3(1)
    event2(2)
    event1(4)
    event4(1)
    event3(2)
    event2(3)
    event5(0)
    conv(0)
    event4(2)
    event3(3)
    event2(4)
    event5(1)
    conv(1)
    event4(3)
    event3(4)
    event5(2)
    conv(2)
    event4(4)
    event5(3)
    conv(3)
    event5(4)
    conv(4)
    for copy in pending:
        copy.wait_send()
    for s in range(STAGES):
        piece_copy(s).wait_send()
    small(lat.at[:, 7], halo.at[0], 0, y_up).wait_send()
    small(lat.at[:, 0], halo.at[1], 1, y_dn).wait_send()
    for k, peer in ((2, y_up), (3, y_dn), (4, y_op)):
        small(stats.at[y], stats.at[y], k, peer).wait_send()


def spatial_section(latents, gain, shift, kernel, bias):
    vmem = pl.BlockSpec(memory_space=pltpu.VMEM)
    anywhere = pl.BlockSpec(memory_space=pl.ANY)
    dma = pltpu.SemaphoreType.DMA
    return pl.pallas_call(
        spatial_kernel_body,
        out_shape=jax.ShapeDtypeStruct((2, 288, C), jnp.bfloat16),
        in_specs=[anywhere, vmem, vmem, anywhere, vmem],
        out_specs=vmem,
        scratch_shapes=[
            pltpu.VMEM((10, 4, 4, 9, 80, 128), jnp.bfloat16),
            pltpu.VMEM((3, 2, 320, C), jnp.bfloat16),
            pltpu.VMEM((LANES, 40 * PITCH, 128), jnp.float32),
            pltpu.VMEM((4, 8, 18, C), jnp.bfloat16),
            pltpu.VMEM((2, 4, 18, C), jnp.bfloat16),
            pltpu.VMEM((2, 288, C), jnp.bfloat16),
            pltpu.VMEM((576, 256), jnp.float32),
            pltpu.VMEM((STAGES, 2, 6, 40, 128), jnp.bfloat16),
            pltpu.VMEM((4, LANES, 8, 128), jnp.float32),
            pltpu.VMEM((LANES, 8, 128), jnp.float32),
            dma((STAGES, KINDS)),
            dma((STAGES, KINDS)),
            dma((STAGES,)),
            dma((STAGES,)),
            dma((STAGES,)),
            dma((5,)),
            dma((5,)),
            dma,
        ],
        compiler_params=pltpu.CompilerParams(
            collective_id=0, has_side_effects=True, vmem_limit_bytes=60 * 1024 * 1024
        ),
        cost_estimate=pl.CostEstimate(
            flops=2 * 576 * 9 * C * C, bytes_accessed=40_000_000, transcendentals=2_000_000
        ),
        name="spatial",
    )(latents, gain[None], shift[None], kernel.reshape(9, 40, C), bias[None])


def body(
    latents,
    first_gain,
    first_shift,
    spatial_kernel,
    spatial_bias,
    second_gain,
    second_shift,
    temporal_kernel,
    temporal_bias,
    frame_slot,
):
    videos = 4
    frame_total = 100
    group_width = 40
    pixel_slots = 5
    spatial = spatial_section(latents, first_gain, first_shift, spatial_kernel, spatial_bias)
    flat = spatial.reshape(144, 4, C)
    flat = jnp.pad(flat, ((0, 16), (0, 0), (0, 0)))
    outgoing = flat.reshape(32, 5, 4, C)
    arrived = lax.all_to_all(outgoing, "frames", split_axis=0, concat_axis=0, tiled=True)
    arrived = arrived.transpose(0, 2, 1, 3).reshape(128, 5, C)
    ordered = arrived[frame_slot].reshape(videos, FRAMES, pixel_slots, C)
    ordered_values = ordered.astype(jnp.float32)
    grouped = ordered_values.reshape(videos, FRAMES * pixel_slots, GROUPS, group_width)
    clip_sum, clip_square = lax.psum(
        (jnp.sum(grouped, axis=(1, 3)), jnp.sum(grouped * grouped, axis=(1, 3))), ("frames", "rows")
    )
    clip_entries = FRAMES * 576 * group_width
    clip_average = (clip_sum / clip_entries)[:, None, :, None]
    clip_squares = (clip_square / clip_entries)[:, None, :, None]
    clip_scaled = (grouped - clip_average) * lax.rsqrt(
        clip_squares - clip_average * clip_average + EPS
    )
    hidden_two = jax.nn.silu(
        clip_scaled.reshape(ordered.shape) * second_gain + second_shift
    ).astype(jnp.bfloat16)
    extended_two = jnp.pad(hidden_two, ((0, 0), (1, 1), (0, 0), (0, 0)))
    temporal = jnp.zeros((videos * FRAMES * pixel_slots, C), jnp.float32)
    for frame_tap in range(3):
        window = extended_two[:, frame_tap : frame_tap + FRAMES].reshape(-1, C)
        temporal = temporal + jnp.dot(
            window, temporal_kernel[frame_tap], preferred_element_type=jnp.float32
        )
    mixed = (ordered_values + temporal.reshape(ordered.shape) + temporal_bias).astype(jnp.bfloat16)
    placed = jnp.zeros((128, pixel_slots, C), jnp.bfloat16)
    placed = placed.at[frame_slot].set(mixed.reshape(frame_total, pixel_slots, C))
    returned = lax.all_to_all(
        placed.reshape(32, 4, pixel_slots, C), "frames", split_axis=0, concat_axis=0, tiled=True
    )
    result = returned.transpose(0, 2, 1, 3).reshape(160, 4, C)[:144]
    result = result.reshape(2, 18, 4, 4, C).transpose(3, 0, 2, 1, 4)
    return result.reshape(latents.shape)


def solution(mesh):
    in_specs = (
        P("frames", "rows", None, None),
        P(),
        P(),
        P(None, None, "frames", None),
        P(),
        P(),
        P(),
        P(),
        P(),
        P(),
    )
    out_specs = P("frames", "rows", None, None)
    return jax.shard_map(body, mesh=mesh, in_specs=in_specs, out_specs=out_specs, check_vma=False)
```

time: 389 us -> 297 us (0.76); the launches traced: 382 us -> 296 us
  Pallas kernels: 0 us -> 93.6 us
  waiting for transfers between devices: 80.1 us -> 22.7 us
  matrix products: 64.6 us -> 13 us
  local copies, waits for them, and re-layouts: 88.6 us -> 57.5 us
  between operations: 13.9 us -> 0.19 us
  other arithmetic: 23 us -> 11.4 us
  blocking collectives: 103 us -> 92.5 us
    pallas_call x0 -> x1, Pallas kernels: none -> 93.6 us  [spatial_section(): pl.pallas_call(spatial_kernel_body, out_shape=jax.ShapeDtypeStruct((2, 28...]
    all_gather x1 -> x0, waiting for transfers between devices: 51.8 us -> none  [body(): whole_kernel = lax.all_gather(spatial_kernel, 'frames', axis=2, tiled=True)]
    dot_general x9 -> x0, matrix products: 51.6 us -> none  [add_taps(): jnp.dot(window, kernel_piece[row_tap, col_tap], preferred_element_type=jn...]
    reshape x14 -> x5, local copies, waits for them, and re-layouts: 38 us -> 11.7 us  [the longest x2 6.25 us: body(): window = extended_two[:, frame_tap:frame_tap + FRAMES].reshape(-1, C)]
    psum x1 -> x0, blocking collectives: 9.56 us -> none  [body(): frame_sum, frame_square = lax.psum((band_sum, band_square), 'rows')]
    slice x6 -> x4, local copies, waits for them, and re-layouts: 13.7 us -> 8.23 us  [the longest x3 7.72 us: body(): window = extended_two[:, frame_tap:frame_tap + FRAMES].reshape(-1, C)]
    concatenate x2 -> x0, other arithmetic: 5.29 us -> none  [extended_2(): block = jnp.concatenate([low, block, high], axis=dim)]
    ppermute x2 -> x0, waiting for transfers between devices: 4.88 us -> none  [the longest x1 4.79 us: extended_2(): lax.ppermute(lax.slice_in_dim(block, 0, width, axis=dim), axis, backward)]
  transfers between devices with their start and end apart: 4 -> 1, of which waited for: 4 -> 1; matrix products, arithmetic and copies ran while one was open for 10% -> 0% of each run, Pallas kernels for 0% -> 0%
where the time goes in v1:
time: 297 us; the launch traced here: 296 us
  Pallas kernels  93.6 us (32%)
  blocking collectives  92.5 us (31%)
  local copies, waits for them, and re-layouts  57.5 us (19%)
  waiting for transfers between devices  22.7 us (8%)
  matrix products  13 us (4%)
  other arithmetic  11.4 us (4%)
  starting transfers between devices  4.72 us (2%)
    pallas_call x1, Pallas kernels, spatial_section(): pl.pallas_call(spatial_kernel_body, out_shape=jax.ShapeDtypeStruct((2, 28...  93.6 us
    psum x1, blocking collectives, body(): lax.psum((jnp.sum(grouped, axis=(1, 3)), jnp.sum(grouped * grouped, axis=...  64.5 us
    all_to_all x1, blocking collectives, body(): lax.all_to_all(placed.reshape(32, 4, pixel_slots, C), 'frames', split_axi...  28 us
    all_to_all x1, waiting for transfers between devices, body(): lax.all_to_all(outgoing, 'frames', split_axis=0, concat_axis=0, tiled=True)  22.7 us
    dot_general x3, matrix products, body(): jnp.dot(window, temporal_kernel[frame_tap], preferred_element_type=jnp.fl...  13 us
    scatter x1, local copies, waits for them, and re-layouts, body(): placed.at[frame_slot].set(mixed.reshape(frame_total, pixel_slots, C))  10.6 us
    slice x3, local copies, waits for them, and re-layouts, body(): window = extended_two[:, frame_tap:frame_tap + FRAMES].reshape(-1, C)  7.72 us
    reshape x2, local copies, waits for them, and re-layouts, body(): window = extended_two[:, frame_tap:frame_tap + FRAMES].reshape(-1, C)  6.25 us
  transfers between devices with their start and end apart: 1, of which 1 were waited for; matrix products, arithmetic and copies ran while one was open for 0% of the time, Pallas kernels for 0%

profile of v1, /device:TPU:1, one launch (start us, length us, event | category | flops | bytes accessed | tf_op | source)
XLA Modules:
  0.0 295.6 jit_solution(136899919377194843)
XLA Ops:
  0.0 0.0 copy-start.5
  0.0 0.0 copy-start.6
  0.0 0.0 copy-start.7
  0.0 3.0 %copy.37.lat = bf16[4,8,18,1280]{3,2,1,0:T(8,128)(2,1)} copy(bf16[4,8,18,1280]{3,1,2,0:T(8,128)(2,1)} %param.10) | data formatting | bytes 2949120 | tf_op args[0]
  3.0 0.0 copy-done.5
  3.0 0.6 broadcast_in_dim.23.gain
  3.6 0.0 copy-done.6
  3.6 0.6 broadcast_in_dim.24.shift
  4.2 0.0 copy-done.7
  4.2 0.6 broadcast_in_dim.25.bias
  4.8 93.6 %spatial.1 = bf16[2,288,1280]{2,1,0:T(8,128)(2,1)} custom-call(bf16[4,8,18,1280]{3,2,1,0:T(8,128)(2,1)} %copy.37.lat, f32[1,1280]{1,0:T(1,128)} %broadcast_in_dim.23.gain, f32[1,1280]{1,0:T(1,128)} %broadcast_in_dim.24.shift, bf16[9,40,1280]{2,1,0:T(8,128)(2,1)} %bitcast.33, f32[1,1280]{1,0:T(1,128)} %broadcast_in_dim.25.bias), custom_call_target="tpu_custom_call" | custom-call | flops 16986931200 | bytes 40000000 | tf_op jit(solution)/shard_map/spatial/pallas_call | solution.py:418
  98.4 2.8 reshape.109
  101.2 0.0 copy-start.8
  101.2 1.8 pad.8
  103.0 4.7 %all-to-all-start = ((bf16[32,5,4,1280]{3,2,1,0:T(4,128)(2,1)}), bf16[32,5,4,1280]{3,2,1,0:T(4,128)(2,1)S(1)}, u32[]{:S(2)}, u32[]{:S(2)}) async-start(bf16[32,5,4,1280]{3,2,1,0:T(4,128)(2,1)} %bitcast.1), calls=%async_computation | async-start | bytes 3276800 | tf_op jit(solution)/shard_map/all_to_all | solution.py:473
  107.7 0.0 copy-done.8
  107.8 22.7 %all-to-all-done = bf16[32,5,4,1280]{3,2,1,0:T(4,128)(2,1)S(1)} async-done(((bf16[32,5,4,1280]{3,2,1,0:T(4,128)(2,1)}), bf16[32,5,4,1280]{3,2,1,0:T(4,128)(2,1)S(1)}, u32[]{:S(2)}, u32[]{:S(2)}) %all-to-all-start) | async-done | bytes 1638432 | tf_op jit(solution)/shard_map/all_to_all | solution.py:473
  130.5 2.0 copy.48
  132.5 2.5 gather_fusion
  135.0 2.5 convert_reduce_fusion
  137.5 2.5 reduce_sum.24
  140.0 2.5 reduce_sum.36
  142.5 1.7 reduce_sum.25
  144.1 1.7 reduce_sum.37
  145.8 64.5 %all-reduce.2 = (f32[4,32]{1,0:T(4,128)S(1)}, f32[4,32]{1,0:T(4,128)S(1)}) all-reduce(f32[4,32]{1,0:T(4,128)S(1)} %reduce_sum.37, f32[4,32]{1,0:T(4,128)S(1)} %reduce_sum.25), channel_id=1, replica_groups=mesh['frames'=32,'rows'=4] {'frames','rows'}, use_global_device_ids=true, to_apply=%region_5.6 | all-reduce | flops 256 | bytes 2048 | tf_op jit(solution)/shard_map/psum | solution.py:478
  210.3 0.1 mul.59
  210.3 0.1 mul.60
  210.4 0.1 sub.25
  210.5 0.1 sub.26
  210.6 0.0 copy-start.2
  210.6 0.0 copy-start.3
  210.7 0.3 convert.2
  211.0 0.4 copy-done.2
  211.3 0.0 copy-done.3
  211.4 1.3 multiply_convert_fusion
  212.6 2.2 pad_slice_fusion
  214.8 2.1 copy.42
  216.9 2.1 copy.41
  218.9 2.6 reshape.112
  221.6 3.6 %convert_element_type.46 = bf16[500,1280]{1,0:T(8,128)(2,1)} reshape(bf16[4,25,5,1280]{3,2,1,0:T(8,128)(2,1)} %copy.42) | data formatting | bytes 2560000 | tf_op jit(solution)/shard_map/convert_element_type | solution.py:489
  225.2 3.5 %copy.43 = bf16[4,25,5,1280]{3,2,1,0:T(8,128)(2,1)} copy(bf16[4,25,5,1280]{3,1,0,2:T(8,128)(2,1)} %get-tuple-element.9) | data formatting | bytes 2560000 | tf_op jit(solution)/shard_map/slice | solution.py:493
  228.7 3.6 %reshape.113 = bf16[500,1280]{1,0:T(8,128)(2,1)} reshape(bf16[4,25,5,1280]{3,2,1,0:T(8,128)(2,1)} %copy.43) | data formatting | bytes 2560000 | tf_op jit(solution)/shard_map/reshape | solution.py:493
  232.3 0.0 copy-start
  232.3 3.9 %fusion.2 = f32[500,1280]{1,0:T(8,128)S(1)} fusion(bf16[500,1280]{1,0:T(8,128)(2,1)S(1)} %reshape.112, bf16[3,1280,1280]{2,1,0:T(8,128)(2,1)} %param.17), kind=kOutput, calls=%fused_computation.8 | convolution fusion | flops 1638400000 | bytes 7116800 | tf_op jit(solution)/shard_map/dot_general | solution.py:494
  236.2 0.0 copy-done
  236.2 0.0 copy-start.1
  236.2 3.9 %convolution_add_fusion.1 = f32[500,1280]{1,0:T(8,128)S(1)} fusion(f32[500,1280]{1,0:T(8,128)S(1)} %fusion.2, bf16[500,1280]{1,0:T(8,128)(2,1)S(1)} %copy-done, bf16[3,1280,1280]{2,1,0:T(8,128)(2,1)} %param.17), kind=kOutput, calls=%fused_computation.5 | convolution fusion | flops 1639040000 | bytes 9676800 | tf_op jit(solution)/shard_map/dot_general | solution.py:494
  240.1 0.0 copy-done.1
  240.1 5.3 %convolution_add_fusion = f32[500,1280]{1,0:T(8,128)} fusion(f32[500,1280]{1,0:T(8,128)S(1)} %convolution_add_fusion.1, bf16[500,1280]{1,0:T(8,128)(2,1)S(1)} %copy-done.1, bf16[3,1280,1280]{2,1,0:T(8,128)(2,1)} %param.17), kind=kOutput, calls=%fused_computation.4 | convolution fusion | flops 1639040000 | bytes 9676800 | tf_op jit(solution)/shard_map/dot_general | solution.py:494
  245.4 0.0 copy-start.4
  245.4 4.3 %reshape.114 = f32[100,5,1280]{2,1,0:T(8,128)} reshape(f32[500,1280]{1,0:T(8,128)} %convolution_add_fusion) | data formatting | bytes 5120000 | tf_op jit(solution)/shard_map/reshape | solution.py:497
  249.7 0.0 copy-done.4
  249.7 4.0 %add_convert_fusion = bf16[100,5,1280]{2,1,0:T(8,128)(2,1)} fusion(f32[100,5,1280]{2,1,0:T(8,128)} %reshape.114, bf16[100,5,1280]{2,1,0:T(8,128)(2,1)S(1)} %gather_fusion, f32[1280]{0:T(1024)S(1)} %copy-done.4), kind=kLoop, calls=%fused_computation.2 | loop fusion | flops 2560000 | bytes 5125120 | tf_op jit(solution)/shard_map/convert_element_type | solution.py:497
  253.7 0.2 broadcast_in_dim.10
  253.9 10.6 %scatter_fusion = bf16[128,5,1280]{2,1,0:T(8,128)(2,1)S(1)} fusion(bf16[128,5,1280]{2,1,0:T(8,128)(2,1)S(1)} %broadcast_in_dim.10, s32[100]{0:T(128)S(1)} %compare_select_fusion, bf16[100,5,1280]{2,1,0:T(8,128)(2,1)} %add_convert_fusion), kind=kCustom, calls=%fused_computation.1 | custom fusion | bytes 3840400 | tf_op jit(solution)/shard_map/scatter | solution.py:499
  264.5 0.7 copy.45
  265.2 28.0 %all_to_all.10 = bf16[32,4,5,1280]{3,1,2,0:T(4,128)(2,1)S(1)} all-to-all(bf16[32,4,5,1280]{3,1,2,0:T(4,128)(2,1)S(1)} %copy.45), channel_id=1, replica_groups=mesh['frames'=32,'rows'=4] {'frames'}, dimensions={0} | all-to-all | bytes 3276800 | tf_op jit(solution)/shard_map/all_to_all | solution.py:500
  293.2 0.5 slice.27
  293.7 0.5 copy.46
  294.2 1.4 copy.47
  (3 shorter events, 0.0 us)
Async XLA Ops:
  0.0 3.0 %copy-start.5 = (f32[1280]{0:T(1024)S(1)}, f32[1280]{0:T(1024)}, u32[]{:S(2)}) copy-start(f32[1280]{0:T(1024)} %param.11) | copy-start | bytes 15364
  0.0 3.6 %copy-start.6 = (f32[1280]{0:T(1024)S(1)}, f32[1280]{0:T(1024)}, u32[]{:S(2)}) copy-start(f32[1280]{0:T(1024)} %param.12) | copy-start | bytes 15364
  0.0 4.2 %copy-start.7 = (f32[1280]{0:T(1024)S(1)}, f32[1280]{0:T(1024)}, u32[]{:S(2)}) copy-start(f32[1280]{0:T(1024)} %param.14) | copy-start | bytes 15364
  101.2 6.5 %copy-start.8 = (s32[100]{0:T(128)S(1)}, s32[100]{0:T(128)}, u32[]{:S(2)}) copy-start(s32[100]{0:T(128)} %param.19) | copy-start | bytes 1204
  103.0 27.5 %all-to-all-start = ((bf16[32,5,4,1280]{3,2,1,0:T(4,128)(2,1)}), bf16[32,5,4,1280]{3,2,1,0:T(4,128)(2,1)S(1)}, u32[]{:S(2)}, u32[]{:S(2)}) async-start(bf16[32,5,4,1280]{3,2,1,0:T(4,128)(2,1)} %bitcast.1), calls=%async_computation | async-start | bytes 3276800 | tf_op jit(solution)/shard_map/all_to_all | solution.py:473
  210.6 0.7 copy-start.2
  210.6 0.7 copy-start.3
  232.3 3.9 %copy-start = (bf16[500,1280]{1,0:T(8,128)(2,1)S(1)}, bf16[500,1280]{1,0:T(8,128)(2,1)}, u32[]{:S(2)}) copy-start(bf16[500,1280]{1,0:T(8,128)(2,1)} %convert_element_type.46) | copy-start | bytes 3840004
  236.2 3.9 %copy-start.1 = (bf16[500,1280]{1,0:T(8,128)(2,1)S(1)}, bf16[500,1280]{1,0:T(8,128)(2,1)}, u32[]{:S(2)}) copy-start(bf16[500,1280]{1,0:T(8,128)(2,1)} %reshape.113) | copy-start | bytes 3840004
  245.4 4.3 %copy-start.4 = (f32[1280]{0:T(1024)S(1)}, f32[1280]{0:T(1024)}, u32[]{:S(2)}) copy-start(f32[1280]{0:T(1024)} %param.18) | copy-start | bytes 15364

commit v2 on v1

--- a/solution.py
+++ b/solution.py
@@ -5,8 +5,6 @@
 from jax.experimental.pallas import tpu as pltpu
 from jax.sharding import PartitionSpec as P
 
-FRAMES = 25
-GROUPS = 32
 EPS = 1e-06
 MESH = pl.DeviceIdType.MESH
 C = 1280
@@ -32,23 +30,66 @@
     return jnp.dot(a, b, preferred_element_type=jnp.float32, precision=lax.Precision.HIGHEST)
 
 
+def iota(shape, dim):
+    return lax.broadcasted_iota(jnp.int32, shape, dim)
+
+
+def flag(mask):
+    return jnp.where(mask, 1.0, 0.0).astype(jnp.bfloat16)
+
+
+def by_slot(total, square):
+    a = (total[0:4] + total[4:8]) + (total[8:12] + total[12:16])
+    b = (square[0:4] + square[4:8]) + (square[8:12] + square[12:16])
+    return jnp.concatenate([a, b], axis=0)
+
+
+def slot_vectors(slots, padded):
+    padded[...] = jnp.full((1, 128), -1, jnp.int32)
+    padded[:, 0:100] = slots[...]
+    row = padded[...].astype(jnp.float32)
+    wide = jnp.broadcast_to(row, (128, 128))
+    diagonal = jnp.where(iota((128, 128), 0) == iota((128, 128), 1), wide, 0.0)
+    return row, jnp.sum(diagonal, axis=1, keepdims=True)
+
+
+def greet_plane(barrier, fr):
+    def one(i, carry):
+        pl.semaphore_signal(
+            barrier, inc=1, device_id={"frames": lax.rem(fr + i, 32)}, device_id_type=MESH
+        )
+        return carry
+
+    lax.fori_loop(1, 32, one, 0)
+
+
 def spatial_kernel_body(
     lat,
     gain,
     shift,
     wk,
     bias,
-    out,
+    slots,
+    A,
+    AX,
+    clip,
     G,
     X,
     F,
     R,
     halo,
     RM,
+    S,
+    EX,
     acc,
     pieces,
     stats,
     scales,
+    slot_sums,
+    slot_sent,
+    slot_all,
+    clip_all,
+    slot_pad,
     send,
     recv,
     piece_send,
@@ -57,6 +98,9 @@
     small_send,
     small_recv,
     lat_sem,
+    a2a_send,
+    a2a_recv,
+    a2a_own,
 ):
     fr = lax.axis_index("frames")
     y = lax.axis_index("rows")
@@ -83,9 +127,10 @@
     y_dn = {"rows": wrap(y - 1)}
     y_op = {"rows": wrap(y + 2)}
     barrier = pltpu.get_barrier_semaphore()
-    for peer in (u_up, u_dn, w_up, w_dn, sib, y_up, y_dn, y_op):
+    for peer in (y_up, y_dn, y_op):
         pl.semaphore_signal(barrier, inc=1, device_id=peer, device_id_type=MESH)
-    pl.semaphore_wait(barrier, 8)
+    greet_plane(barrier, fr)
+    pl.semaphore_wait(barrier, 34)
 
     plane_tap = 3 * par
 
@@ -251,9 +296,127 @@
         lax.fori_loop(0, 3, one, 0)
         cols = slice(256 * s, 256 * s + 256)
         base = RM[:, :, cols].reshape(576, 256).astype(jnp.float32)
-        out[:, :, cols] = (
-            (base + acc[...] + bias[:, cols]).astype(jnp.bfloat16).reshape(2, 288, 256)
-        )
+        value = base + acc[...] + bias[:, cols]
+        value = jnp.where(jnp.abs(value) < 3.3e38, value, 0.0).astype(jnp.bfloat16)
+        S[:, :, cols] = value.reshape(36, 16, 256)
+        value = value.astype(jnp.float32).reshape(36, 16, 256)
+        total = jnp.sum(value, axis=0)
+        square = jnp.sum(value * value, axis=0)
+        slot_sums[2 * s] = by_slot(total[:, 0:128], square[:, 0:128])
+        slot_sums[2 * s + 1] = by_slot(total[:, 128:256], square[:, 128:256])
+
+    def send_tiles(k, lo, hi):
+        def one(i, carry):
+            d = lax.rem(fr + i, 32)
+            pltpu.make_async_remote_copy(
+                src_ref=S.at[d, :, lo:hi],
+                dst_ref=A.at[fr, :, lo:hi],
+                send_sem=a2a_send.at[k],
+                recv_sem=a2a_recv.at[k],
+                device_id={"frames": d},
+                device_id_type=MESH,
+            ).start()
+            return carry
+
+        lax.fori_loop(1, 32, one, 0)
+        pltpu.make_async_copy(S.at[fr, :, lo:hi], A.at[fr, :, lo:hi], a2a_own.at[k]).start()
+
+    def wait_tiles(k, lo, hi):
+        pltpu.make_async_copy(S.at[fr, :, lo:hi], A.at[fr, :, lo:hi], a2a_own.at[k]).wait()
+        wait_all(S.at[0:31, :, lo:hi], A.at[0:31, :, lo:hi], k)
+
+    def wait_all(src, dst, k):
+        both = pltpu.make_async_remote_copy(
+            src_ref=src,
+            dst_ref=dst,
+            send_sem=a2a_send.at[k],
+            recv_sem=a2a_recv.at[k],
+            device_id=sib,
+            device_id_type=MESH,
+        )
+        both.wait_send()
+        both.wait_recv()
+
+    def send_extra():
+        for t in range(4):
+            for l in range(LANES):
+                part = S[32 + t, :, l * 128 : l * 128 + 128].astype(jnp.float32)
+                stacks[t][l] = part
+        for t in range(4):
+            for r in range(4):
+                for m in range(3):
+                    picked = [
+                        stacks[t][l][4 * r : 4 * r + 4]
+                        if l < LANES
+                        else jnp.zeros((4, 128), jnp.float32)
+                        for l in range(4 * m, 4 * m + 4)
+                    ]
+                    EX[4 * t + r, m] = jnp.concatenate(picked, axis=0).astype(jnp.bfloat16)
+
+        def one(i, carry):
+            d = lax.rem(fr + i, 32)
+            pltpu.make_async_remote_copy(
+                src_ref=EX.at[lax.div(d, 2)],
+                dst_ref=AX.at[fr],
+                send_sem=a2a_send.at[3],
+                recv_sem=a2a_recv.at[3],
+                device_id={"frames": d},
+                device_id_type=MESH,
+            ).start()
+            return carry
+
+        lax.fori_loop(1, 32, one, 0)
+        pltpu.make_async_copy(EX.at[chip], AX.at[fr], a2a_own.at[3]).start()
+
+    def send_sums():
+        grouped = jnp.zeros((8, 128), jnp.float32)
+        for l in range(LANES):
+            grouped = grouped + exact_dot(slot_sums[l], group_indicator(l))
+        grouped = jnp.minimum(jnp.maximum(grouped, -3e38), 3e38)
+        slot_sent[...] = grouped
+        slot_all[fr] = grouped
+
+        def one(i, carry):
+            d = lax.rem(fr + i, 32)
+            pltpu.make_async_remote_copy(
+                src_ref=slot_sent,
+                dst_ref=slot_all.at[fr],
+                send_sem=a2a_send.at[4],
+                recv_sem=a2a_recv.at[4],
+                device_id={"frames": d},
+                device_id_type=MESH,
+            ).start()
+            return carry
+
+        lax.fori_loop(1, 32, one, 0)
+
+    def clip_copy(k, peer):
+        return small(clip_all.at[y], clip_all.at[y], k, peer)
+
+    def clip_sums():
+        wait_all(slot_all.at[0:31], slot_all.at[0:31], 4)
+        row, col = slot_vectors(slots, slot_pad)
+        kind = lax.shift_right_logical(iota((8, 128), 0), 2)
+        video = jnp.bitwise_and(iota((8, 128), 0), 3) * 25
+        j = iota((8, 128), 1)
+        pick = flag((j >= video) & (j < video + 25))
+        entry = iota((128, 256), 1)
+        slot_of = lax.shift_right_logical(entry, 3) * 4 + jnp.bitwise_and(entry, 3)
+        match = flag(col == slot_of.astype(jnp.float32))
+        pick = jnp.dot(pick, match, preferred_element_type=jnp.float32)
+        same = jnp.bitwise_and(lax.shift_right_logical(iota((8, 256), 1), 2), 1) == (
+            lax.shift_right_logical(iota((8, 256), 0), 2)
+        )
+        pick = jnp.where(same, pick, 0.0)
+        clip_all[y] = exact_dot(pick, slot_all[...].reshape(256, 128))
+        for k, peer in ((5, y_up), (6, y_dn), (7, y_op)):
+            clip_copy(k, peer).start()
+        for k, o, peer in ((5, 3, y_up), (6, 1, y_dn), (7, 2, y_op)):
+            source = clip_all.at[wrap(y + o)]
+            small(source, source, k, peer).wait_recv()
+        clip[...] = (clip_all[0] + clip_all[1]) + (clip_all[2] + clip_all[3])
+
+    stacks = [[None] * LANES for _ in range(4)]
 
     def raw_rows():
         lat_copy.wait()
@@ -392,6 +555,7 @@
     event2(4)
     event5(1)
     conv(1)
+    send_tiles(0, 0, 512)
     event4(3)
     event3(4)
     event5(2)
@@ -399,8 +563,29 @@
     event4(4)
     event5(3)
     conv(3)
+    send_tiles(1, 512, 1024)
     event5(4)
     conv(4)
+    send_sums()
+    send_tiles(2, 1024, 1280)
+    send_extra()
+    clip_sums()
+    wait_tiles(0, 0, 512)
+    wait_tiles(1, 512, 1024)
+    wait_tiles(2, 1024, 1280)
+    pltpu.make_async_copy(EX.at[chip], AX.at[fr], a2a_own.at[3]).wait()
+    rest = pltpu.make_async_remote_copy(
+        src_ref=AX.at[0:31],
+        dst_ref=AX.at[0:31],
+        send_sem=a2a_send.at[3],
+        recv_sem=a2a_recv.at[3],
+        device_id=sib,
+        device_id_type=MESH,
+    )
+    rest.wait_send()
+    rest.wait_recv()
+    for k, peer in ((5, y_up), (6, y_dn), (7, y_op)):
+        clip_copy(k, peer).wait_send()
     for copy in pending:
         copy.wait_send()
     for s in range(STAGES):
@@ -411,15 +596,19 @@
         small(stats.at[y], stats.at[y], k, peer).wait_send()
 
 
-def spatial_section(latents, gain, shift, kernel, bias):
+def spatial_section(latents, gain, shift, kernel, bias, slots):
     vmem = pl.BlockSpec(memory_space=pltpu.VMEM)
     anywhere = pl.BlockSpec(memory_space=pl.ANY)
     dma = pltpu.SemaphoreType.DMA
     return pl.pallas_call(
         spatial_kernel_body,
-        out_shape=jax.ShapeDtypeStruct((2, 288, C), jnp.bfloat16),
-        in_specs=[anywhere, vmem, vmem, anywhere, vmem],
-        out_specs=vmem,
+        out_shape=(
+            jax.ShapeDtypeStruct((32, 16, C), jnp.bfloat16),
+            jax.ShapeDtypeStruct((32, 3, 16, 128), jnp.bfloat16),
+            jax.ShapeDtypeStruct((8, 128), jnp.float32),
+        ),
+        in_specs=[anywhere, vmem, vmem, anywhere, vmem, vmem],
+        out_specs=(vmem, vmem, vmem),
         scratch_shapes=[
             pltpu.VMEM((10, 4, 4, 9, 80, 128), jnp.bfloat16),
             pltpu.VMEM((3, 2, 320, C), jnp.bfloat16),
@@ -427,18 +616,28 @@
             pltpu.VMEM((4, 8, 18, C), jnp.bfloat16),
             pltpu.VMEM((2, 4, 18, C), jnp.bfloat16),
             pltpu.VMEM((2, 288, C), jnp.bfloat16),
+            pltpu.VMEM((36, 16, C), jnp.bfloat16),
+            pltpu.VMEM((16, 3, 16, 128), jnp.bfloat16),
             pltpu.VMEM((576, 256), jnp.float32),
             pltpu.VMEM((STAGES, 2, 6, 40, 128), jnp.bfloat16),
             pltpu.VMEM((4, LANES, 8, 128), jnp.float32),
             pltpu.VMEM((LANES, 8, 128), jnp.float32),
+            pltpu.VMEM((LANES, 8, 128), jnp.float32),
+            pltpu.VMEM((8, 128), jnp.float32),
+            pltpu.VMEM((32, 8, 128), jnp.float32),
+            pltpu.VMEM((4, 8, 128), jnp.float32),
+            pltpu.VMEM((1, 128), jnp.int32),
             dma((STAGES, KINDS)),
             dma((STAGES, KINDS)),
             dma((STAGES,)),
             dma((STAGES,)),
             dma((STAGES,)),
+            dma((8,)),
+            dma((8,)),
+            dma,
             dma((5,)),
             dma((5,)),
-            dma,
+            dma((4,)),
         ],
         compiler_params=pltpu.CompilerParams(
             collective_id=0, has_side_effects=True, vmem_limit_bytes=60 * 1024 * 1024
@@ -447,7 +646,254 @@
             flops=2 * 576 * 9 * C * C, bytes_accessed=40_000_000, transcendentals=2_000_000
         ),
         name="spatial",
-    )(latents, gain[None], shift[None], kernel.reshape(9, 40, C), bias[None])
+    )(latents, gain[None], shift[None], kernel.reshape(9, 40, C), bias[None], slots[None])
+
+
+def temporal_kernel_body(
+    A,
+    AX,
+    clip,
+    slots,
+    wt,
+    gain,
+    shift,
+    bias,
+    O,
+    W,
+    H,
+    RF,
+    HE,
+    RE,
+    OM,
+    OX,
+    BX,
+    back,
+    back_extra,
+    scale_rows,
+    slot_pad,
+    w_sem,
+    send,
+    recv,
+    own,
+):
+    fr = lax.axis_index("frames")
+    core = lax.rem(fr, 2)
+    sib = {"frames": fr + 1 - 2 * core}
+    loads = [
+        pltpu.make_async_copy(
+            wt.at[:, :, 256 * n : 256 * n + 256], W.at[:, :, 256 * n : 256 * n + 256], w_sem.at[n]
+        )
+        for n in range(5)
+    ]
+    for load in loads:
+        load.start()
+    barrier = pltpu.get_barrier_semaphore()
+    greet_plane(barrier, fr)
+
+    row, col = slot_vectors(slots, slot_pad)
+
+    def entry_slot(entry):
+        return lax.shift_right_logical(entry, 4) * 4 + jnp.bitwise_and(entry, 3)
+
+    def entry_pixel(entry):
+        return jnp.bitwise_and(lax.shift_right_logical(entry, 2), 3)
+
+    match = flag(col == entry_slot(iota((128, 512), 1)).astype(jnp.float32))
+    match_t = flag(entry_slot(iota((512, 128), 0)).astype(jnp.float32) == row)
+
+    def frame_number(line, shift_bits):
+        frame = lax.shift_right_logical(line, shift_bits)
+        video = jnp.bitwise_and(lax.shift_right_logical(line, shift_bits - 2), 3)
+        return video * 25 + frame
+
+    def real(line, count):
+        return line < count
+
+    line = iota((400, 128), 0)
+    which = flag(frame_number(line, 4) == iota((400, 128), 1))
+    pick = jnp.dot(which, match, preferred_element_type=jnp.float32)
+    pixel = jnp.bitwise_and(iota((400, 512), 0), 3)
+    pick = jnp.where(pixel == entry_pixel(iota((400, 512), 1)), pick, 0.0).astype(jnp.bfloat16)
+    line_t = iota((128, 400), 1)
+    which_t = flag(frame_number(line_t, 4) == iota((128, 400), 0))
+    pick_t = jnp.dot(match_t, which_t, preferred_element_type=jnp.float32)
+    pixel_t = jnp.bitwise_and(iota((512, 400), 1), 3)
+    back[...] = jnp.where(pixel_t == entry_pixel(iota((512, 400), 0)), pick_t, 0.0).astype(
+        jnp.bfloat16
+    )
+    line = iota((112, 128), 0)
+    which = flag((frame_number(line, 2) == iota((112, 128), 1)) & (line < 100))
+    extra = jnp.dot(which, match, preferred_element_type=jnp.float32)
+    extra_pixel = entry_pixel(iota((112, 512), 1))
+    line_t = iota((128, 112), 1)
+    which_t = flag((frame_number(line_t, 2) == iota((128, 112), 0)) & (line_t < 100))
+    extra_t = jnp.dot(match_t, which_t, preferred_element_type=jnp.float32)
+    extra_pixel_t = entry_pixel(iota((512, 112), 0))
+    for i in range(4):
+        back_extra[i] = jnp.where(extra_pixel_t == i, extra_t, 0.0).astype(jnp.bfloat16)
+    for n in range(5):
+        cols = slice(256 * n, 256 * n + 256)
+        RF[:, cols] = jnp.dot(
+            pick, A[:, :, cols].reshape(512, 256), preferred_element_type=jnp.float32
+        ).astype(jnp.bfloat16)
+    for i in range(4):
+        picked = jnp.where(extra_pixel == i, extra, 0.0).astype(jnp.bfloat16)
+        for m in range(3):
+            l = 4 * m + i
+            if l < LANES:
+                RE[:, l * 128 : l * 128 + 128] = jnp.dot(
+                    picked, AX[:, m].reshape(512, 128), preferred_element_type=jnp.float32
+                ).astype(jnp.bfloat16)
+
+    grouped = clip[...] * (1.0 / 576000.0)
+    mean = grouped[0:4]
+    rate = lax.rsqrt(grouped[4:8] - mean * mean + EPS)
+    both = jnp.concatenate([rate, mean * rate], axis=0)
+    HE[0:8, :] = jnp.zeros((8, C), jnp.float32)
+    HE[104:128, :] = jnp.zeros((24, C), jnp.float32)
+    H[0] = jnp.zeros((16, C), jnp.bfloat16)
+    H[26] = jnp.zeros((16, C), jnp.bfloat16)
+    for l in range(LANES):
+        cols = slice(l * 128, l * 128 + 128)
+        wide = exact_dot(both, group_indicator_t(l))
+        a = wide[0:4] * gain[:, cols]
+        b = shift[:, cols] - wide[4:8] * gain[:, cols]
+        for o, part in ((0, a), (16, b)):
+            scale_rows[o : o + 16, cols] = jnp.concatenate(
+                [jnp.broadcast_to(part[v : v + 1], (4, 128)) for v in range(4)], axis=0
+            )
+        a8 = jnp.concatenate([a, a], axis=0)
+        b8 = jnp.concatenate([b, b], axis=0)
+        raw = RE[:, cols].astype(jnp.float32).reshape(14, 8, 128)
+        v = raw * a8[None] + b8[None]
+        v = (v * (1.0 / (1.0 + jnp.exp(-v)))).reshape(112, 128)
+        HE[8:108, cols] = v[0:100]
+
+    def one(f, carry):
+        for l in range(LANES):
+            cols = slice(l * 128, l * 128 + 128)
+            v = RF[pl.ds(pl.multiple_of(f * 16, 16), 16), cols].astype(jnp.float32)
+            v = v * scale_rows[0:16, cols] + scale_rows[16:32, cols]
+            v = v * (1.0 / (1.0 + jnp.exp(-v)))
+            H[f + 1, :, cols] = v.astype(jnp.bfloat16)
+        return carry
+
+    lax.fori_loop(0, 25, one, 0)
+    pl.semaphore_wait(barrier, 31)
+
+    def spread(src, dst, k):
+        def one(i, carry):
+            d = lax.rem(fr + i, 32)
+            pltpu.make_async_remote_copy(
+                src_ref=src(d),
+                dst_ref=dst(fr),
+                send_sem=send.at[k],
+                recv_sem=recv.at[k],
+                device_id={"frames": d},
+                device_id_type=MESH,
+            ).start()
+            return carry
+
+        lax.fori_loop(1, 32, one, 0)
+        pltpu.make_async_copy(src(fr), dst(fr), own.at[k]).start()
+
+    def collect(src, dst, k):
+        pltpu.make_async_copy(src(fr), dst(fr), own.at[k]).wait()
+        whole = pltpu.make_async_remote_copy(
+            src_ref=src(slice(0, 31)),
+            dst_ref=dst(slice(0, 31)),
+            send_sem=send.at[k],
+            recv_sem=recv.at[k],
+            device_id=sib,
+            device_id_type=MESH,
+        )
+        whole.wait_send()
+        whole.wait_recv()
+
+    def chunk(n):
+        cols = slice(256 * n, 256 * n + 256)
+        return (lambda d: OM.at[d, :, cols]), (lambda d: O.at[d, :, cols])
+
+    for n in range(5):
+        cols = slice(256 * n, 256 * n + 256)
+        loads[n].wait()
+        total = RF[:, cols].astype(jnp.float32) + bias[:, cols]
+        for k in range(3):
+            total = total + jnp.dot(
+                H[k : k + 25].reshape(400, C), W[k, :, cols], preferred_element_type=jnp.float32
+            )
+        placed = jnp.dot(back[...], total.astype(jnp.bfloat16), preferred_element_type=jnp.float32)
+        OM[:, :, cols] = placed.astype(jnp.bfloat16).reshape(32, 16, 256)
+        spread(*chunk(n), n)
+    half = pl.multiple_of(core * 640, 128)
+    total = RE[:, pl.ds(half, 640)].astype(jnp.float32) + bias[:, pl.ds(half, 640)]
+    for k in range(3):
+        window = HE[4 + 4 * k : 116 + 4 * k, :].astype(jnp.bfloat16)
+        total = total + jnp.dot(
+            window, W[k, :, pl.ds(half, 640)], preferred_element_type=jnp.float32
+        )
+    mixed = total.astype(jnp.bfloat16)
+    for m in range(2):
+        placed = jnp.zeros((512, 128), jnp.float32)
+        for i in range(4):
+            l = 4 * m + i
+            if l < 5:
+                placed = placed + jnp.dot(
+                    back_extra[i],
+                    mixed[:, l * 128 : l * 128 + 128],
+                    preferred_element_type=jnp.float32,
+                )
+        OX[:, m] = placed.astype(jnp.bfloat16).reshape(32, 16, 128)
+    spread((lambda d: OX.at[d]), (lambda d: BX.at[d]), 5)
+    collect((lambda d: OX.at[d]), (lambda d: BX.at[d]), 5)
+    for t in range(4):
+        for l in range(LANES):
+            k, m, i = l // 5, (l % 5) // 4, (l % 5) % 4
+            part = [
+                BX[2 * (4 * t + r) + k, m].astype(jnp.float32)[4 * i : 4 * i + 4] for r in range(4)
+            ]
+            O[32 + t, :, l * 128 : l * 128 + 128] = jnp.concatenate(part, axis=0).astype(
+                jnp.bfloat16
+            )
+    for n in range(5):
+        collect(*chunk(n), n)
+
+
+def temporal_section(A, AX, clip, slots, kernel, gain, shift, bias):
+    vmem = pl.BlockSpec(memory_space=pltpu.VMEM)
+    anywhere = pl.BlockSpec(memory_space=pl.ANY)
+    dma = pltpu.SemaphoreType.DMA
+    return pl.pallas_call(
+        temporal_kernel_body,
+        out_shape=jax.ShapeDtypeStruct((36, 16, C), jnp.bfloat16),
+        in_specs=[vmem, vmem, vmem, vmem, anywhere, vmem, vmem, vmem],
+        out_specs=vmem,
+        scratch_shapes=[
+            pltpu.VMEM((3, C, C), jnp.bfloat16),
+            pltpu.VMEM((27, 16, C), jnp.bfloat16),
+            pltpu.VMEM((400, C), jnp.bfloat16),
+            pltpu.VMEM((128, C), jnp.float32),
+            pltpu.VMEM((112, C), jnp.bfloat16),
+            pltpu.VMEM((32, 16, C), jnp.bfloat16),
+            pltpu.VMEM((32, 2, 16, 128), jnp.bfloat16),
+            pltpu.VMEM((32, 2, 16, 128), jnp.bfloat16),
+            pltpu.VMEM((512, 400), jnp.bfloat16),
+            pltpu.VMEM((4, 512, 112), jnp.bfloat16),
+            pltpu.VMEM((32, C), jnp.float32),
+            pltpu.VMEM((1, 128), jnp.int32),
+            dma((5,)),
+            dma((6,)),
+            dma((6,)),
+            dma((6,)),
+        ],
+        compiler_params=pltpu.CompilerParams(
+            collective_id=1, has_side_effects=True, vmem_limit_bytes=56 * 1024 * 1024
+        ),
+        cost_estimate=pl.CostEstimate(
+            flops=2 * 500 * 3 * C * C, bytes_accessed=14_000_000, transcendentals=1_000_000
+        ),
+        name="temporal",
+    )(A, AX, clip, slots[None], kernel, gain[None], shift[None], bias[None])
 
 
 def body(
@@ -462,46 +908,13 @@
     temporal_bias,
     frame_slot,
 ):
-    videos = 4
-    frame_total = 100
-    group_width = 40
-    pixel_slots = 5
-    spatial = spatial_section(latents, first_gain, first_shift, spatial_kernel, spatial_bias)
-    flat = spatial.reshape(144, 4, C)
-    flat = jnp.pad(flat, ((0, 16), (0, 0), (0, 0)))
-    outgoing = flat.reshape(32, 5, 4, C)
-    arrived = lax.all_to_all(outgoing, "frames", split_axis=0, concat_axis=0, tiled=True)
-    arrived = arrived.transpose(0, 2, 1, 3).reshape(128, 5, C)
-    ordered = arrived[frame_slot].reshape(videos, FRAMES, pixel_slots, C)
-    ordered_values = ordered.astype(jnp.float32)
-    grouped = ordered_values.reshape(videos, FRAMES * pixel_slots, GROUPS, group_width)
-    clip_sum, clip_square = lax.psum(
-        (jnp.sum(grouped, axis=(1, 3)), jnp.sum(grouped * grouped, axis=(1, 3))), ("frames", "rows")
+    main, extra, clip = spatial_section(
+        latents, first_gain, first_shift, spatial_kernel, spatial_bias, frame_slot
     )
-    clip_entries = FRAMES * 576 * group_width
-    clip_average = (clip_sum / clip_entries)[:, None, :, None]
-    clip_squares = (clip_square / clip_entries)[:, None, :, None]
-    clip_scaled = (grouped - clip_average) * lax.rsqrt(
-        clip_squares - clip_average * clip_average + EPS
+    tiles = temporal_section(
+        main, extra, clip, frame_slot, temporal_kernel, second_gain, second_shift, temporal_bias
     )
-    hidden_two = jax.nn.silu(
-        clip_scaled.reshape(ordered.shape) * second_gain + second_shift
-    ).astype(jnp.bfloat16)
-    extended_two = jnp.pad(hidden_two, ((0, 0), (1, 1), (0, 0), (0, 0)))
-    temporal = jnp.zeros((videos * FRAMES * pixel_slots, C), jnp.float32)
-    for frame_tap in range(3):
-        window = extended_two[:, frame_tap : frame_tap + FRAMES].reshape(-1, C)
-        temporal = temporal + jnp.dot(
-            window, temporal_kernel[frame_tap], preferred_element_type=jnp.float32
-        )
-    mixed = (ordered_values + temporal.reshape(ordered.shape) + temporal_bias).astype(jnp.bfloat16)
-    placed = jnp.zeros((128, pixel_slots, C), jnp.bfloat16)
-    placed = placed.at[frame_slot].set(mixed.reshape(frame_total, pixel_slots, C))
-    returned = lax.all_to_all(
-        placed.reshape(32, 4, pixel_slots, C), "frames", split_axis=0, concat_axis=0, tiled=True
-    )
-    result = returned.transpose(0, 2, 1, 3).reshape(160, 4, C)[:144]
-    result = result.reshape(2, 18, 4, 4, C).transpose(3, 0, 2, 1, 4)
+    result = tiles.reshape(2, 18, 4, 4, C).transpose(3, 0, 2, 1, 4)
     return result.reshape(latents.shape)
 
 

time: 297 us -> 151 us (0.51)
  blocking collectives: 92.5 us -> 0 us
  local copies, waits for them, and re-layouts: 57.5 us -> 11.3 us
  Pallas kernels: 93.6 us -> 139 us
  waiting for transfers between devices: 22.7 us -> 0 us
  matrix products: 13 us -> 0 us
  other arithmetic: 11.4 us -> 0 us
  starting transfers between devices: 4.72 us -> 0 us
    psum x1 -> x0, blocking collectives: 64.5 us -> none  [body(): lax.psum((jnp.sum(grouped, axis=(1, 3)), jnp.sum(grouped * grouped, axis=...]
    pallas_call x1 -> x2, Pallas kernels: 93.6 us -> 139 us  [the longest x1 110 us: spatial_section(): pl.pallas_call(spatial_kernel_body, out_shape=(jax.ShapeDtypeStruct((32,...]
    all_to_all x1 -> x0, blocking collectives: 28 us -> none  [body(): lax.all_to_all(placed.reshape(32, 4, pixel_slots, C), 'frames', split_axi...]
    all_to_all x1 -> x0, waiting for transfers between devices: 22.7 us -> none  [body(): lax.all_to_all(outgoing, 'frames', split_axis=0, concat_axis=0, tiled=True)]
    reshape x6 -> x1, local copies, waits for them, and re-layouts: 16 us -> 2.79 us  [body(): result = tiles.reshape(2, 18, 4, 4, C).transpose(3, 0, 2, 1, 4)]
    dot_general x3 -> x0, matrix products: 13 us -> none  [body(): jnp.dot(window, temporal_kernel[frame_tap], preferred_element_type=jnp.fl...]
    scatter x1 -> x0, local copies, waits for them, and re-layouts: 10.6 us -> none  [body(): placed.at[frame_slot].set(mixed.reshape(frame_total, pixel_slots, C))]
    slice x4 -> x0, local copies, waits for them, and re-layouts: 8.23 us -> none  [the longest x3 7.72 us: body(): window = extended_two[:, frame_tap:frame_tap + FRAMES].reshape(-1, C)]
  transfers between devices with their start and end apart: 1 -> 0, of which waited for: 1 -> 0; matrix products, arithmetic and copies ran while one was open for 0% -> 0% of each run, Pallas kernels for 0% -> 0%
where the time goes in v2:
time: 151 us
  Pallas kernels  139 us (92%)
  local copies, waits for them, and re-layouts  11.3 us (7%)
    pallas_call x1, Pallas kernels, spatial_section(): pl.pallas_call(spatial_kernel_body, out_shape=(jax.ShapeDtypeStruct((32,...  110 us
    pallas_call x1, Pallas kernels, temporal_section(): pl.pallas_call(temporal_kernel_body, out_shape=jax.ShapeDtypeStruct((36,...  29.1 us
    unnamed x13, local copies, waits for them, and re-layouts  3.06 us

profile of v2, /device:TPU:1, one launch (start us, length us, event | category | flops | bytes accessed | tf_op | source)
XLA Modules:
  0.0 150.6 jit_solution(11347099710882169015)
XLA Ops:
  0.0 0.0 copy-start
  0.0 0.0 copy-start.1
  0.0 0.0 copy-start.2
  0.0 3.0 %copy.11.lat = bf16[4,8,18,1280]{3,2,1,0:T(8,128)(2,1)} copy(bf16[4,8,18,1280]{3,1,2,0:T(8,128)(2,1)} %param.10) | data formatting | bytes 2949120 | tf_op args[0]
  3.0 0.0 copy-done
  3.0 0.6 broadcast_in_dim.22.gain
  3.6 0.0 copy-done.1
  3.6 0.6 broadcast_in_dim.23.shift
  4.2 0.0 copy-done.2
  4.3 0.6 broadcast_in_dim.24.bias
  4.8 0.0 copy-start.3
  4.8 0.0 copy-start.4
  4.9 0.0 copy-start.5
  4.9 110.1 %spatial.1 = (bf16[32,16,1280]{2,1,0:T(8,128)(2,1)}, bf16[32,3,16,128]{3,2,1,0:T(8,128)(2,1)}, f32[8,128]{1,0:T(8,128)}) custom-call(bf16[4,8,18,1280]{3,2,1,0:T(8,128)(2,1)} %copy.11.lat, f32[1,1280]{1,0:T(1,128)} %broadcast_in_dim.22.gain, f32[1,1280]{1,0:T(1,128)} %broadcast_in_dim.23.shift, bf16[9,40,1280]{2,1,0:T(8,128)(2,1)} %bitcast.6, ...), custom_call_target="tpu_custom_call" | custom-call | flops 16986931200 | bytes 40000000 | tf_op jit(solution)/shard_map/spatial/pallas_call | solution.py:603
  115.0 0.0 copy-done.3
  115.0 0.6 broadcast_in_dim.26.gain
  115.6 0.0 copy-done.4
  115.6 0.6 broadcast_in_dim.27.shift
  116.2 0.0 copy-done.5
  116.2 0.6 broadcast_in_dim.28.bias
  116.8 29.1 %temporal.1 = bf16[36,16,1280]{2,1,0:T(8,128)(2,1)} custom-call(bf16[32,16,1280]{2,1,0:T(8,128)(2,1)} %get-tuple-element.8.A, bf16[32,3,16,128]{3,2,1,0:T(8,128)(2,1)} %get-tuple-element.9.AX, f32[8,128]{1,0:T(8,128)} %get-tuple-element.10.clip, s32[1,100]{1,0:T(1,128)} %bitcast.8, bf16[3,1280,1280]{2,1,0:T(8,128)(2,1)} %wt.1, ...), custom_call_target="tpu_custom_call" | custom-call | flops 4915200000 | bytes 14000000 | tf_op jit(solution)/shard_map/temporal/pallas_call | solution.py:866
  145.9 2.8 %reshape.10 = bf16[2,18,4,4,1280]{4,3,2,1,0:T(4,128)(2,1)S(1)} reshape(bf16[36,16,1280]{2,1,0:T(8,128)(2,1)} %temporal.1) | data formatting | bytes 2949120 | tf_op jit(solution)/shard_map/reshape | solution.py:917
  148.7 0.6 copy.12
  149.3 1.3 reshape.11
Async XLA Ops:
  0.0 3.0 %copy-start = (f32[1280]{0:T(1024)S(1)}, f32[1280]{0:T(1024)}, u32[]{:S(2)}) copy-start(f32[1280]{0:T(1024)} %param.11) | copy-start | bytes 15364
  0.0 3.6 %copy-start.1 = (f32[1280]{0:T(1024)S(1)}, f32[1280]{0:T(1024)}, u32[]{:S(2)}) copy-start(f32[1280]{0:T(1024)} %param.12) | copy-start | bytes 15364
  0.0 4.2 %copy-start.2 = (f32[1280]{0:T(1024)S(1)}, f32[1280]{0:T(1024)}, u32[]{:S(2)}) copy-start(f32[1280]{0:T(1024)} %param.14) | copy-start | bytes 15364
  4.8 110.2 %copy-start.3 = (f32[1280]{0:T(1024)S(1)}, f32[1280]{0:T(1024)}, u32[]{:S(2)}) copy-start(f32[1280]{0:T(1024)} %param.15) | copy-start | bytes 15364
  4.8 110.8 %copy-start.4 = (f32[1280]{0:T(1024)S(1)}, f32[1280]{0:T(1024)}, u32[]{:S(2)}) copy-start(f32[1280]{0:T(1024)} %param.16) | copy-start | bytes 15364
  4.9 111.4 %copy-start.5 = (f32[1280]{0:T(1024)S(1)}, f32[1280]{0:T(1024)}, u32[]{:S(2)}) copy-start(f32[1280]{0:T(1024)} %param.18) | copy-start | bytes 15364

commit v3 on v2

--- a/solution.py
+++ b/solution.py
@@ -10,24 +10,44 @@
 C = 1280
 LANES = 10
 STAGES = 5
-PITCH = 24
 KINDS = 24
 
 
-def group_indicator(tile):
-    channel = lax.broadcasted_iota(jnp.int32, (128, 128), 0) + tile * 128
-    first = lax.broadcasted_iota(jnp.int32, (128, 128), 1) * 40
-    return jnp.where((channel >= first) & (channel < first + 40), 1.0, 0.0)
-
-
-def group_indicator_t(tile):
-    channel = lax.broadcasted_iota(jnp.int32, (128, 128), 1) + tile * 128
-    first = lax.broadcasted_iota(jnp.int32, (128, 128), 0) * 40
-    return jnp.where((channel >= first) & (channel < first + 40), 1.0, 0.0)
+def member(shape, channel_dim):
+    channel = iota(shape, channel_dim)
+    first = iota(shape, 1 - channel_dim) * 40
+    return flag((channel >= first) & (channel < first + 40))
 
 
 def exact_dot(a, b):
-    return jnp.dot(a, b, preferred_element_type=jnp.float32, precision=lax.Precision.HIGHEST)
+    rows = a.shape[0]
+    high = a.astype(jnp.bfloat16)
+    rest = a - high.astype(jnp.float32)
+    middle = rest.astype(jnp.bfloat16)
+    low = (rest - middle.astype(jnp.float32)).astype(jnp.bfloat16)
+    parts = jnp.concatenate([high.astype(jnp.float32), middle.astype(jnp.float32), low.astype(jnp.float32)], axis=0)
+    out = jnp.dot(parts.astype(jnp.bfloat16), b, preferred_element_type=jnp.float32)
+    return (out[2 * rows :] + out[rows : 2 * rows]) + out[0:rows]
+
+
+def exact_pick(pick, b):
+    pick = pick.astype(jnp.bfloat16)
+    high = b.astype(jnp.bfloat16)
+    rest = b - high.astype(jnp.float32)
+    middle = rest.astype(jnp.bfloat16)
+    low = (rest - middle.astype(jnp.float32)).astype(jnp.bfloat16)
+    out = jnp.dot(
+        pick, jnp.concatenate([high, middle, low], axis=1), preferred_element_type=jnp.float32
+    )
+    return (out[:, 256:384] + out[:, 128:256]) + out[:, 0:128]
+
+
+def to_groups(tiles):
+    return exact_dot(jnp.concatenate(tiles, axis=1), member((C, 128), 0))
+
+
+def to_channels(groups):
+    return exact_dot(groups, member((128, C), 1))
 
 
 def iota(shape, dim):
@@ -77,7 +97,8 @@
     X,
     F,
     R,
-    halo,
+    edge_out,
+    edge_in,
     RM,
     S,
     EX,
@@ -110,7 +131,7 @@
     z = lax.div(chip, 4)
     u = x + core * (z - x)
     w = z + core * (x - z)
-    par = lax.rem(y, 2)
+    part = lax.rem(y, 2)
 
     def wrap(v):
         return lax.rem(v + 4, 4)
@@ -130,13 +151,17 @@
     for peer in (y_up, y_dn, y_op):
         pl.semaphore_signal(barrier, inc=1, device_id=peer, device_id_type=MESH)
     greet_plane(barrier, fr)
-    pl.semaphore_wait(barrier, 34)
-
-    plane_tap = 3 * par
+    lat_copy = pltpu.make_async_copy(lat, R, lat_sem)
+    lat_copy.start()
+
+    plane_tap = 3 * part
+
+    def piece_cols(s, c):
+        return pl.ds(pl.multiple_of(256 * s + 128 * c, 128), 128)
 
     def piece_copy(s):
         return pltpu.make_async_remote_copy(
-            src_ref=wk.at[pl.ds(plane_tap, 6), :, pl.ds(pl.multiple_of(256 * s + 128 * (1 - core), 128), 128)],
+            src_ref=wk.at[pl.ds(plane_tap, 6), :, piece_cols(s, 1 - core)],
             dst_ref=pieces.at[s, core],
             send_sem=piece_send.at[s],
             recv_sem=piece_recv.at[s],
@@ -156,16 +181,14 @@
 
     def piece_local(s):
         return pltpu.make_async_copy(
-            wk.at[pl.ds(plane_tap, 6), :, pl.ds(pl.multiple_of(256 * s + 128 * core, 128), 128)],
-            pieces.at[s, core],
-            piece_own.at[s],
-        )
-
+            wk.at[pl.ds(plane_tap, 6), :, piece_cols(s, core)], pieces.at[s, core], piece_own.at[s]
+        )
+
+    for s in range(STAGES):
+        piece_local(s).start()
+    pl.semaphore_wait(barrier, 34)
     for s in range(STAGES):
         piece_copy(s).start()
-        piece_local(s).start()
-    lat_copy = pltpu.make_async_copy(lat, R, lat_sem)
-    lat_copy.start()
 
     def small(src, dst, k, target):
         return pltpu.make_async_remote_copy(
@@ -177,9 +200,6 @@
             device_id_type=MESH,
         )
 
-    small(lat.at[:, 7], halo.at[0], 0, y_up).start()
-    small(lat.at[:, 0], halo.at[1], 1, y_dn).start()
-
     def region(q, row, u0, count, tap, taps):
         return G.at[q, row, pl.ds(u0, count), pl.ds(tap, taps)]
 
@@ -195,8 +215,8 @@
 
     rows = [w, wrap(w - 1), wrap(w + 1), wrap(w + 2)]
     sib_rows = [u, wrap(u - 1), wrap(u + 1), wrap(u + 2)]
-    out_tap = 6 * par
-    in_tap = 6 * (1 - par)
+    out_tap = 6 * part
+    in_tap = 6 * (1 - part)
     pending = []
 
     def go(k, s, ref, target):
@@ -279,8 +299,6 @@
             arrived(20 + i, s, region(q, sib_rows[i], 0, 4, in_tap, 3), sib)
 
     def conv(s):
-        acc[...] = jnp.zeros_like(acc)
-
         def one(a, carry):
             for b in range(3):
                 t = a * 3 + b
@@ -293,37 +311,46 @@
                 acc[...] += jnp.dot(window, kernel, preferred_element_type=jnp.float32)
             return carry
 
+        acc[...] = jnp.zeros_like(acc)
         lax.fori_loop(0, 3, one, 0)
-        cols = slice(256 * s, 256 * s + 256)
-        base = RM[:, :, cols].reshape(576, 256).astype(jnp.float32)
-        value = base + acc[...] + bias[:, cols]
-        value = jnp.where(jnp.abs(value) < 3.3e38, value, 0.0).astype(jnp.bfloat16)
-        S[:, :, cols] = value.reshape(36, 16, 256)
-        value = value.astype(jnp.float32).reshape(36, 16, 256)
-        total = jnp.sum(value, axis=0)
-        square = jnp.sum(value * value, axis=0)
-        slot_sums[2 * s] = by_slot(total[:, 0:128], square[:, 0:128])
-        slot_sums[2 * s + 1] = by_slot(total[:, 128:256], square[:, 128:256])
-
-    def send_tiles(k, lo, hi):
+        for n in range(2):
+            q = 2 * s + n
+            base = RM[:, q].reshape(576, 128).astype(jnp.float32)
+            value = base + acc[:, 128 * n : 128 * n + 128]
+            value = value + bias[q * 128 : q * 128 + 128].reshape(1, 128)
+            value = jnp.where(jnp.abs(value) < 3.3e38, value, 0.0).astype(jnp.bfloat16)
+            S[:, q] = value.reshape(36, 16, 128)
+
+    def each_peer(start):
         def one(i, carry):
-            d = lax.rem(fr + i, 32)
-            pltpu.make_async_remote_copy(
-                src_ref=S.at[d, :, lo:hi],
-                dst_ref=A.at[fr, :, lo:hi],
-                send_sem=a2a_send.at[k],
-                recv_sem=a2a_recv.at[k],
+            start(lax.rem(fr + i, 32))
+            return carry
+
+        lax.fori_loop(1, 32, one, 0)
+
+    def finish(s):
+        span = slice(2 * s, 2 * s + 2)
+        each_peer(
+            lambda d: pltpu.make_async_remote_copy(
+                src_ref=S.at[d, span],
+                dst_ref=A.at[fr, span],
+                send_sem=a2a_send.at[s],
+                recv_sem=a2a_recv.at[s],
                 device_id={"frames": d},
                 device_id_type=MESH,
             ).start()
-            return carry
-
-        lax.fori_loop(1, 32, one, 0)
-        pltpu.make_async_copy(S.at[fr, :, lo:hi], A.at[fr, :, lo:hi], a2a_own.at[k]).start()
-
-    def wait_tiles(k, lo, hi):
-        pltpu.make_async_copy(S.at[fr, :, lo:hi], A.at[fr, :, lo:hi], a2a_own.at[k]).wait()
-        wait_all(S.at[0:31, :, lo:hi], A.at[0:31, :, lo:hi], k)
+        )
+        pltpu.make_async_copy(S.at[fr, span], A.at[fr, span], a2a_own.at[s]).start()
+        if s in (1, 3, 4):
+            send_extra(s // 2)
+        for q in range(2 * s, 2 * s + 2):
+            value = S[:, q].astype(jnp.float32)
+            slot_sums[q] = by_slot(jnp.sum(value, axis=0), jnp.sum(value * value, axis=0))
+
+    def wait_tiles(s):
+        span = slice(2 * s, 2 * s + 2)
+        pltpu.make_async_copy(S.at[fr, span], A.at[fr, span], a2a_own.at[s]).wait()
+        wait_all(S.at[0:31, span], A.at[0:31, span], s)
 
     def wait_all(src, dst, k):
         both = pltpu.make_async_remote_copy(
@@ -337,64 +364,48 @@
         both.wait_send()
         both.wait_recv()
 
-    def send_extra():
+    def send_extra(m):
         for t in range(4):
-            for l in range(LANES):
-                part = S[32 + t, :, l * 128 : l * 128 + 128].astype(jnp.float32)
-                stacks[t][l] = part
-        for t in range(4):
+            lanes = [S[32 + t, q].astype(jnp.float32) for q in range(4 * m, min(4 * m + 4, LANES))]
             for r in range(4):
-                for m in range(3):
-                    picked = [
-                        stacks[t][l][4 * r : 4 * r + 4]
-                        if l < LANES
-                        else jnp.zeros((4, 128), jnp.float32)
-                        for l in range(4 * m, 4 * m + 4)
-                    ]
-                    EX[4 * t + r, m] = jnp.concatenate(picked, axis=0).astype(jnp.bfloat16)
-
-        def one(i, carry):
-            d = lax.rem(fr + i, 32)
-            pltpu.make_async_remote_copy(
-                src_ref=EX.at[lax.div(d, 2)],
-                dst_ref=AX.at[fr],
-                send_sem=a2a_send.at[3],
-                recv_sem=a2a_recv.at[3],
+                picked = [v[4 * r : 4 * r + 4] for v in lanes]
+                picked += [jnp.zeros((4, 128), jnp.float32)] * (4 - len(lanes))
+                EX[4 * t + r, m] = jnp.concatenate(picked, axis=0).astype(jnp.bfloat16)
+        each_peer(
+            lambda d: pltpu.make_async_remote_copy(
+                src_ref=EX.at[lax.div(d, 2), m],
+                dst_ref=AX.at[fr, m],
+                send_sem=a2a_send.at[5 + m],
+                recv_sem=a2a_recv.at[5 + m],
                 device_id={"frames": d},
                 device_id_type=MESH,
             ).start()
-            return carry
-
-        lax.fori_loop(1, 32, one, 0)
-        pltpu.make_async_copy(EX.at[chip], AX.at[fr], a2a_own.at[3]).start()
+        )
+        pltpu.make_async_copy(EX.at[chip, m], AX.at[fr, m], a2a_own.at[5 + m]).start()
+
+    def wait_extra(m):
+        pltpu.make_async_copy(EX.at[chip, m], AX.at[fr, m], a2a_own.at[5 + m]).wait()
+        wait_all(AX.at[0:31, m], AX.at[0:31, m], 5 + m)
 
     def send_sums():
-        grouped = jnp.zeros((8, 128), jnp.float32)
-        for l in range(LANES):
-            grouped = grouped + exact_dot(slot_sums[l], group_indicator(l))
+        grouped = to_groups([slot_sums[l] for l in range(LANES)])
         grouped = jnp.minimum(jnp.maximum(grouped, -3e38), 3e38)
         slot_sent[...] = grouped
         slot_all[fr] = grouped
 
-        def one(i, carry):
-            d = lax.rem(fr + i, 32)
-            pltpu.make_async_remote_copy(
+        each_peer(
+            lambda d: pltpu.make_async_remote_copy(
                 src_ref=slot_sent,
                 dst_ref=slot_all.at[fr],
-                send_sem=a2a_send.at[4],
-                recv_sem=a2a_recv.at[4],
+                send_sem=a2a_send.at[8],
+                recv_sem=a2a_recv.at[8],
                 device_id={"frames": d},
                 device_id_type=MESH,
             ).start()
-            return carry
-
-        lax.fori_loop(1, 32, one, 0)
-
-    def clip_copy(k, peer):
-        return small(clip_all.at[y], clip_all.at[y], k, peer)
+        )
 
     def clip_sums():
-        wait_all(slot_all.at[0:31], slot_all.at[0:31], 4)
+        wait_all(slot_all.at[0:31], slot_all.at[0:31], 8)
         row, col = slot_vectors(slots, slot_pad)
         kind = lax.shift_right_logical(iota((8, 128), 0), 2)
         video = jnp.bitwise_and(iota((8, 128), 0), 3) * 25
@@ -408,37 +419,44 @@
             lax.shift_right_logical(iota((8, 256), 0), 2)
         )
         pick = jnp.where(same, pick, 0.0)
-        clip_all[y] = exact_dot(pick, slot_all[...].reshape(256, 128))
+        clip_all[y] = exact_pick(pick, slot_all[...].reshape(256, 128))
         for k, peer in ((5, y_up), (6, y_dn), (7, y_op)):
-            clip_copy(k, peer).start()
+            small(clip_all.at[y], clip_all.at[y], k, peer).start()
         for k, o, peer in ((5, 3, y_up), (6, 1, y_dn), (7, 2, y_op)):
             source = clip_all.at[wrap(y + o)]
             small(source, source, k, peer).wait_recv()
         clip[...] = (clip_all[0] + clip_all[1]) + (clip_all[2] + clip_all[3])
 
-    stacks = [[None] * LANES for _ in range(4)]
-
-    def raw_rows():
+    def own_rows():
         lat_copy.wait()
 
-        def one(r, carry):
+        def fill(c, carry):
             for s in range(4):
-                start = pl.multiple_of(((r + 1) * 4 + s) * PITCH, 8)
                 for l in range(LANES):
-                    F[l, pl.ds(start, 18), :] = R[s, r, :, l * 128 : l * 128 + 128].astype(
-                        jnp.float32
-                    )
+                    F[l, c, pl.ds(4 + s, 8, stride=4), :] = R[
+                        s, c, :, l * 128 : l * 128 + 128
+                    ].astype(jnp.float32)
             return carry
 
-        lax.fori_loop(0, 8, one, 0)
+        lax.fori_loop(0, 18, fill, 0)
+
+        def edges(l, carry):
+            edge_out[0, l] = F[l, :, 32:36, :].astype(jnp.bfloat16)
+            edge_out[1, l] = F[l, :, 4:8, :].astype(jnp.bfloat16)
+            return carry
+
+        lax.fori_loop(0, LANES, edges, 0)
+        small(edge_out.at[0], edge_in.at[0], 0, y_up).start()
+        small(edge_out.at[1], edge_in.at[1], 1, y_dn).start()
 
         def sums(l, carry):
+            cols = pl.ds(pl.multiple_of(l * 128, 128), 128)
             total, square = [], []
             for s in range(4):
-                a = jnp.zeros((18, 128), jnp.float32)
-                b = jnp.zeros((18, 128), jnp.float32)
-                for r in range(8):
-                    v = F[l, ((r + 1) * 4 + s) * PITCH : ((r + 1) * 4 + s) * PITCH + 18, :]
+                a = jnp.zeros((8, 128), jnp.float32)
+                b = jnp.zeros((8, 128), jnp.float32)
+                for c in range(18):
+                    v = R[s, c, :, cols].astype(jnp.float32)
                     a = a + v
                     b = b + v * v
                 total.append(jnp.sum(a, axis=0, keepdims=True))
@@ -450,150 +468,124 @@
         for k, peer in ((2, y_up), (3, y_dn), (4, y_op)):
             small(stats.at[y], stats.at[y], k, peer).start()
 
-    def residual_rows():
-        def one(c, carry):
-            for l in range(LANES):
-                for h in range(2):
-                    v = F[l, pl.ds(4 * (4 * h + 1) * PITCH + c, 16, stride=PITCH), :]
-                    RM[h, pl.ds(pl.multiple_of(c * 16, 16), 16), l * 128 : l * 128 + 128] = (
-                        v.astype(jnp.bfloat16)
-                    )
-            return carry
-
-        lax.fori_loop(0, 18, one, 0)
-
-    def hidden_rows():
-        small(lat.at[:, 7], halo.at[0], 0, y_up).wait_recv()
-        small(lat.at[:, 0], halo.at[1], 1, y_dn).wait_recv()
-        for side, r in ((0, 0), (1, 9)):
-            for s in range(4):
-                start = (r * 4 + s) * PITCH
-                for l in range(LANES):
-                    F[l, start : start + 18, :] = halo[
-                        side, s, :, l * 128 : l * 128 + 128
-                    ].astype(jnp.float32)
-        small(stats.at[wrap(y - 1)], stats.at[wrap(y - 1)], 2, y_up).wait_recv()
-        small(stats.at[wrap(y + 1)], stats.at[wrap(y + 1)], 3, y_dn).wait_recv()
-        small(stats.at[wrap(y + 2)], stats.at[wrap(y + 2)], 4, y_op).wait_recv()
-        grouped = jnp.zeros((8, 128), jnp.float32)
-        for l in range(LANES):
-            total = (stats[0, l] + stats[1, l]) + (stats[2, l] + stats[3, l])
-            grouped = grouped + exact_dot(total, group_indicator(l))
+    def norm_scales():
+        for k, o, peer in ((2, 3, y_up), (3, 1, y_dn), (4, 2, y_op)):
+            source = stats.at[wrap(y + o)]
+            small(source, source, k, peer).wait_recv()
+        grouped = to_groups(
+            [(stats[0, l] + stats[1, l]) + (stats[2, l] + stats[3, l]) for l in range(LANES)]
+        )
         grouped = grouped * (1.0 / 23040.0)
         mean = grouped[0:4]
         rate = lax.rsqrt(grouped[4:8] - mean * mean + EPS)
         both = jnp.concatenate([rate, mean * rate], axis=0)
+        channels = to_channels(both)
         for l in range(LANES):
-            wide = exact_dot(both, group_indicator_t(l))
-            g = gain[:, l * 128 : l * 128 + 128]
-            b = shift[:, l * 128 : l * 128 + 128]
-            scales[l] = jnp.concatenate([wide[0:4] * g, b - wide[4:8] * g], axis=0)
-
-        def one(r, carry):
-            inside = jnp.logical_and(
-                jnp.logical_or(r > 0, y > 0), jnp.logical_or(r < 9, y < 3)
-            )
-            keep = jnp.where(inside, 1.0, 0.0)
-            for s in range(4):
-                start = pl.multiple_of((r * 4 + s) * PITCH, 8)
-                for l in range(LANES):
-                    v = F[l, pl.ds(start, PITCH), :] * scales[l, s : s + 1] + scales[
-                        l, 4 + s : 5 + s
-                    ]
-                    v = v * (1.0 / (1.0 + jnp.exp(-v)))
-                    F[l, pl.ds(start, PITCH), :] = jnp.where(keep > 0.5, v, 0.0)
+            wide = channels[:, l * 128 : l * 128 + 128]
+            g = gain[l * 128 : l * 128 + 128].reshape(1, 128)
+            b = shift[l * 128 : l * 128 + 128].reshape(1, 128)
+            up = wide[0:4] * g
+            down = b - wide[4:8] * g
+            scales[l] = jnp.concatenate([up, up, down, down], axis=0)
+
+    def edge_rows():
+        small(edge_out.at[0], edge_in.at[0], 0, y_up).wait_recv()
+        small(edge_out.at[1], edge_in.at[1], 1, y_dn).wait_recv()
+
+        def one(l, carry):
+            F[l, :, 0:4, :] = edge_in[0, l].astype(jnp.float32)
+            F[l, :, 36:40, :] = edge_in[1, l].astype(jnp.float32)
             return carry
 
-        lax.fori_loop(0, 10, one, 0)
+        lax.fori_loop(0, LANES, one, 0)
 
     def window_rows():
-        zero = jnp.zeros((16, C), jnp.bfloat16)
-        for a in range(3):
-            for h in range(2):
-                X[a, h, 0:16, :] = zero
-                X[a, h, 304:320, :] = zero
+        first = jnp.where(y == 0, 4, 0)
+        last = jnp.where(y == 3, 36, 40)
 
         def one(c, carry):
+            line = iota((40, 128), 0)
+            inside = (line >= first) & (line < last)
+            at = pl.ds(pl.multiple_of(c * 16 + 16, 16), 16)
+            here_at = pl.ds(pl.multiple_of(c * 16, 16), 16)
             for l in range(LANES):
+                raw = F[l, c]
+                for h in range(2):
+                    RM[h, l, here_at, :] = raw[16 * h + 4 : 16 * h + 20].astype(jnp.bfloat16)
+                v = raw.reshape(5, 8, 128) * scales[l, 0:8][None] + scales[l, 8:16][None]
+                v = (v * (1.0 / (1.0 + jnp.exp(-v)))).reshape(40, 128)
+                v = jnp.where(inside, v, 0.0)
                 for h in range(2):
                     for a in range(3):
-                        v = F[l, pl.ds(4 * (4 * h + a) * PITCH + c, 16, stride=PITCH), :]
-                        X[
-                            a,
-                            h,
-                            pl.ds(pl.multiple_of(c * 16 + 16, 16), 16),
-                            l * 128 : l * 128 + 128,
-                        ] = v.astype(jnp.bfloat16)
+                        X[a, h, at, l * 128 : l * 128 + 128] = v[
+                            16 * h + 4 * a : 16 * h + 4 * a + 16
+                        ].astype(jnp.bfloat16)
             return carry
 
         lax.fori_loop(0, 18, one, 0)
 
     for s in range(STAGES):
         event0(s)
-    raw_rows()
+    zero = jnp.zeros((16, C), jnp.bfloat16)
+    for a in range(3):
+        for h in range(2):
+            X[a, h, 0:16, :] = zero
+            X[a, h, 304:320, :] = zero
     event1(0)
     event1(1)
-    residual_rows()
     event2(0)
+    own_rows()
     event1(2)
-    hidden_rows()
+    event2(1)
     event3(0)
-    event2(1)
     event1(3)
+    norm_scales()
+    edge_rows()
+    event2(2)
+    event3(1)
+    event4(0)
+    event1(4)
     window_rows()
-    event4(0)
-    event3(1)
-    event2(2)
-    event1(4)
+    event2(3)
+    event3(2)
     event4(1)
-    event3(2)
-    event2(3)
     event5(0)
     conv(0)
+    finish(0)
+    event2(4)
+    event3(3)
     event4(2)
-    event3(3)
-    event2(4)
     event5(1)
     conv(1)
-    send_tiles(0, 0, 512)
+    finish(1)
+    event3(4)
     event4(3)
-    event3(4)
     event5(2)
     conv(2)
+    finish(2)
     event4(4)
     event5(3)
     conv(3)
-    send_tiles(1, 512, 1024)
+    finish(3)
     event5(4)
     conv(4)
+    finish(4)
     send_sums()
-    send_tiles(2, 1024, 1280)
-    send_extra()
     clip_sums()
-    wait_tiles(0, 0, 512)
-    wait_tiles(1, 512, 1024)
-    wait_tiles(2, 1024, 1280)
-    pltpu.make_async_copy(EX.at[chip], AX.at[fr], a2a_own.at[3]).wait()
-    rest = pltpu.make_async_remote_copy(
-        src_ref=AX.at[0:31],
-        dst_ref=AX.at[0:31],
-        send_sem=a2a_send.at[3],
-        recv_sem=a2a_recv.at[3],
-        device_id=sib,
-        device_id_type=MESH,
-    )
-    rest.wait_send()
-    rest.wait_recv()
-    for k, peer in ((5, y_up), (6, y_dn), (7, y_op)):
-        clip_copy(k, peer).wait_send()
+    for s in range(STAGES):
+        wait_tiles(s)
+    for m in range(3):
+        wait_extra(m)
     for copy in pending:
         copy.wait_send()
     for s in range(STAGES):
         piece_copy(s).wait_send()
-    small(lat.at[:, 7], halo.at[0], 0, y_up).wait_send()
-    small(lat.at[:, 0], halo.at[1], 1, y_dn).wait_send()
+    small(edge_out.at[0], edge_in.at[0], 0, y_up).wait_send()
+    small(edge_out.at[1], edge_in.at[1], 1, y_dn).wait_send()
     for k, peer in ((2, y_up), (3, y_dn), (4, y_op)):
         small(stats.at[y], stats.at[y], k, peer).wait_send()
+    for k, peer in ((5, y_up), (6, y_dn), (7, y_op)):
+        small(clip_all.at[y], clip_all.at[y], k, peer).wait_send()
 
 
 def spatial_section(latents, gain, shift, kernel, bias, slots):
@@ -603,25 +595,26 @@
     return pl.pallas_call(
         spatial_kernel_body,
         out_shape=(
-            jax.ShapeDtypeStruct((32, 16, C), jnp.bfloat16),
+            jax.ShapeDtypeStruct((32, LANES, 16, 128), jnp.bfloat16),
             jax.ShapeDtypeStruct((32, 3, 16, 128), jnp.bfloat16),
             jax.ShapeDtypeStruct((8, 128), jnp.float32),
         ),
         in_specs=[anywhere, vmem, vmem, anywhere, vmem, vmem],
         out_specs=(vmem, vmem, vmem),
         scratch_shapes=[
-            pltpu.VMEM((10, 4, 4, 9, 80, 128), jnp.bfloat16),
+            pltpu.VMEM((2 * STAGES, 4, 4, 9, 80, 128), jnp.bfloat16),
             pltpu.VMEM((3, 2, 320, C), jnp.bfloat16),
-            pltpu.VMEM((LANES, 40 * PITCH, 128), jnp.float32),
-            pltpu.VMEM((4, 8, 18, C), jnp.bfloat16),
-            pltpu.VMEM((2, 4, 18, C), jnp.bfloat16),
-            pltpu.VMEM((2, 288, C), jnp.bfloat16),
-            pltpu.VMEM((36, 16, C), jnp.bfloat16),
+            pltpu.VMEM((LANES, 18, 40, 128), jnp.float32),
+            pltpu.VMEM((4, 18, 8, C), jnp.bfloat16),
+            pltpu.VMEM((2, LANES, 18, 4, 128), jnp.bfloat16),
+            pltpu.VMEM((2, LANES, 18, 4, 128), jnp.bfloat16),
+            pltpu.VMEM((2, LANES, 288, 128), jnp.bfloat16),
+            pltpu.VMEM((36, LANES, 16, 128), jnp.bfloat16),
             pltpu.VMEM((16, 3, 16, 128), jnp.bfloat16),
             pltpu.VMEM((576, 256), jnp.float32),
             pltpu.VMEM((STAGES, 2, 6, 40, 128), jnp.bfloat16),
             pltpu.VMEM((4, LANES, 8, 128), jnp.float32),
-            pltpu.VMEM((LANES, 8, 128), jnp.float32),
+            pltpu.VMEM((LANES, 16, 128), jnp.float32),
             pltpu.VMEM((LANES, 8, 128), jnp.float32),
             pltpu.VMEM((8, 128), jnp.float32),
             pltpu.VMEM((32, 8, 128), jnp.float32),
@@ -635,9 +628,9 @@
             dma((8,)),
             dma((8,)),
             dma,
-            dma((5,)),
-            dma((5,)),
-            dma((4,)),
+            dma((9,)),
+            dma((9,)),
+            dma((8,)),
         ],
         compiler_params=pltpu.CompilerParams(
             collective_id=0, has_side_effects=True, vmem_limit_bytes=60 * 1024 * 1024
@@ -646,7 +639,9 @@
             flops=2 * 576 * 9 * C * C, bytes_accessed=40_000_000, transcendentals=2_000_000
         ),
         name="spatial",
-    )(latents, gain[None], shift[None], kernel.reshape(9, 40, C), bias[None], slots[None])
+    )(
+        latents.transpose(0, 2, 1, 3), gain, shift, kernel.reshape(9, 40, C), bias, slots[None]
+    )
 
 
 def temporal_kernel_body(
@@ -732,15 +727,16 @@
     for i in range(4):
         back_extra[i] = jnp.where(extra_pixel_t == i, extra_t, 0.0).astype(jnp.bfloat16)
     for n in range(5):
-        cols = slice(256 * n, 256 * n + 256)
-        RF[:, cols] = jnp.dot(
-            pick, A[:, :, cols].reshape(512, 256), preferred_element_type=jnp.float32
-        ).astype(jnp.bfloat16)
+        both = jnp.concatenate(
+            [A[:, 2 * n].reshape(512, 128), A[:, 2 * n + 1].reshape(512, 128)], axis=1
+        )
+        both = jnp.dot(pick, both, preferred_element_type=jnp.float32).astype(jnp.bfloat16)
+        RF[:, n * 256 : n * 256 + 256] = both
     for i in range(4):
         picked = jnp.where(extra_pixel == i, extra, 0.0).astype(jnp.bfloat16)
         for m in range(3):
-            l = 4 * m + i
-            if l < LANES:
+            if 4 * m + i < LANES:
+                l = 4 * m + i
                 RE[:, l * 128 : l * 128 + 128] = jnp.dot(
                     picked, AX[:, m].reshape(512, 128), preferred_element_type=jnp.float32
                 ).astype(jnp.bfloat16)
@@ -753,11 +749,12 @@
     HE[104:128, :] = jnp.zeros((24, C), jnp.float32)
     H[0] = jnp.zeros((16, C), jnp.bfloat16)
     H[26] = jnp.zeros((16, C), jnp.bfloat16)
+    channels = to_channels(both)
     for l in range(LANES):
         cols = slice(l * 128, l * 128 + 128)
-        wide = exact_dot(both, group_indicator_t(l))
-        a = wide[0:4] * gain[:, cols]
-        b = shift[:, cols] - wide[4:8] * gain[:, cols]
+        wide = channels[:, cols]
+        a = wide[0:4] * gain[cols].reshape(1, 128)
+        b = shift[cols].reshape(1, 128) - wide[4:8] * gain[cols].reshape(1, 128)
         for o, part in ((0, a), (16, b)):
             scale_rows[o : o + 16, cols] = jnp.concatenate(
                 [jnp.broadcast_to(part[v : v + 1], (4, 128)) for v in range(4)], axis=0
@@ -817,7 +814,7 @@
     for n in range(5):
         cols = slice(256 * n, 256 * n + 256)
         loads[n].wait()
-        total = RF[:, cols].astype(jnp.float32) + bias[:, cols]
+        total = RF[:, cols].astype(jnp.float32) + bias[cols].reshape(1, 256)
         for k in range(3):
             total = total + jnp.dot(
                 H[k : k + 25].reshape(400, C), W[k, :, cols], preferred_element_type=jnp.float32
@@ -826,7 +823,7 @@
         OM[:, :, cols] = placed.astype(jnp.bfloat16).reshape(32, 16, 256)
         spread(*chunk(n), n)
     half = pl.multiple_of(core * 640, 128)
-    total = RE[:, pl.ds(half, 640)].astype(jnp.float32) + bias[:, pl.ds(half, 640)]
+    total = RE[:, pl.ds(half, 640)].astype(jnp.float32) + bias[pl.ds(half, 640)].reshape(1, 640)
     for k in range(3):
         window = HE[4 + 4 * k : 116 + 4 * k, :].astype(jnp.bfloat16)
         total = total + jnp.dot(
@@ -893,7 +890,7 @@
             flops=2 * 500 * 3 * C * C, bytes_accessed=14_000_000, transcendentals=1_000_000
         ),
         name="temporal",
-    )(A, AX, clip, slots[None], kernel, gain[None], shift[None], bias[None])
+    )(A, AX, clip, slots[None], kernel, gain, shift, bias)
 
 
 def body(

time: 151 us -> 141 us (0.934)
  local copies, waits for them, and re-layouts: 11.3 us -> 4.66 us
  Pallas kernels: 139 us -> 136 us
    broadcast_in_dim x6 -> x0, local copies, waits for them, and re-layouts: 3.58 us -> none  [the longest x1 0.6 us: temporal_section(): shift[None]]
    pallas_call x1, Pallas kernels: 110 us -> 107 us  [spatial_section(): pl.pallas_call(spatial_kernel_body, out_shape=(jax.ShapeDtypeStruct((32,...]
    unnamed x13 -> x0, local copies, waits for them, and re-layouts: 3.06 us -> none
where the time goes in v3:
time: 141 us
  Pallas kernels  136 us (96%)
  local copies, waits for them, and re-layouts  4.66 us (3%)
    pallas_call x1, Pallas kernels, spatial_section(): pl.pallas_call(spatial_kernel_body, out_shape=(jax.ShapeDtypeStruct((32,...  107 us
    pallas_call x1, Pallas kernels, temporal_section(): pl.pallas_call(temporal_kernel_body, out_shape=jax.ShapeDtypeStruct((36,...  29.2 us

profile of v3, /device:TPU:1, one launch (start us, length us, event | category | flops | bytes accessed | tf_op | source)
XLA Modules:
  0.0 140.6 jit_solution(12584525324137577358)
XLA Ops:
  0.0 106.6 %spatial.1 = (bf16[32,10,16,128]{3,2,1,0:T(8,128)(2,1)}, bf16[32,3,16,128]{3,2,1,0:T(8,128)(2,1)}, f32[8,128]{1,0:T(8,128)}) custom-call(bf16[4,18,8,1280]{3,2,1,0:T(8,128)(2,1)} %bitcast.7, f32[1280]{0:T(1024)} %gain.2, f32[1280]{0:T(1024)} %shift.2, bf16[9,40,1280]{2,1,0:T(8,128)(2,1)} %bitcast.8, f32[1280]{0:T(1024)} %bias.2, s32[1,100]{1,0:T(1,128)} %bitcast.9), custom_call_target="tpu_custom_call" | custom-call | flops 16986931200 | bytes 40000000 | tf_op jit(solution)/shard_map/spatial/pallas_call | solution.py:595
  106.6 29.2 %temporal.1 = bf16[36,16,1280]{2,1,0:T(8,128)(2,1)} custom-call(bf16[32,10,16,128]{3,2,1,0:T(8,128)(2,1)} %get-tuple-element.8.A, bf16[32,3,16,128]{3,2,1,0:T(8,128)(2,1)} %get-tuple-element.9.AX, f32[8,128]{1,0:T(8,128)} %get-tuple-element.10.clip, s32[1,100]{1,0:T(1,128)} %bitcast.10, bf16[3,1280,1280]{2,1,0:T(8,128)(2,1)} %wt.1, f32[1280]{0:T(1024)} %gain.3, ...), custom_call_target="tpu_custom_call" | custom-call | flops 4915200000 | bytes 14000000 | tf_op jit(solution)/shard_map/temporal/pallas_call | solution.py:863
  135.9 2.8 %reshape.10 = bf16[2,18,4,4,1280]{4,3,2,1,0:T(4,128)(2,1)S(1)} reshape(bf16[36,16,1280]{2,1,0:T(8,128)(2,1)} %temporal.1) | data formatting | bytes 2949120 | tf_op jit(solution)/shard_map/reshape | solution.py:914
  138.7 0.6 copy.11
  139.3 1.3 reshape.11

commit v4 on v3

--- a/solution.py
+++ b/solution.py
@@ -31,7 +31,6 @@
 
 
 def exact_pick(pick, b):
-    pick = pick.astype(jnp.bfloat16)
     high = b.astype(jnp.bfloat16)
     rest = b - high.astype(jnp.float32)
     middle = rest.astype(jnp.bfloat16)
@@ -42,8 +41,8 @@
     return (out[:, 256:384] + out[:, 128:256]) + out[:, 0:128]
 
 
-def to_groups(tiles):
-    return exact_dot(jnp.concatenate(tiles, axis=1), member((C, 128), 0))
+def to_groups(tiles, groups_of):
+    return exact_dot(jnp.concatenate(tiles, axis=1), groups_of)
 
 
 def to_channels(groups):
@@ -111,6 +110,8 @@
     slot_all,
     clip_all,
     slot_pad,
+    groups_of,
+    clip_pick,
     send,
     recv,
     piece_send,
@@ -296,23 +297,33 @@
         q = 2 * s + 1 - core
         for i in range(4):
             arrived(16 + i, s, region(q, sib_rows[i], 0, 4, plane_tap, 6), sib)
+
+    def event6(s):
+        q = 2 * s + 1 - core
+        for i in range(4):
             arrived(20 + i, s, region(q, sib_rows[i], 0, 4, in_tap, 3), sib)
 
+    def taps(s, a):
+        for b in range(3):
+            t = a * 3 + b
+            even = G[2 * s, :, :, t].reshape(C, 128)
+            odd = jnp.concatenate(
+                [G[2 * s + 1, i, j, t] for j in range(4) for i in range(4)], axis=0
+            )
+            kernel = jnp.concatenate([even, odd], axis=1)
+            window = X[a, :, b * 16 : b * 16 + 288, :].reshape(576, C)
+            acc[...] += jnp.dot(window, kernel, preferred_element_type=jnp.float32)
+
     def conv(s):
-        def one(a, carry):
-            for b in range(3):
-                t = a * 3 + b
-                even = G[2 * s, :, :, t].reshape(C, 128)
-                odd = jnp.concatenate(
-                    [G[2 * s + 1, i, j, t] for j in range(4) for i in range(4)], axis=0
-                )
-                kernel = jnp.concatenate([even, odd], axis=1)
-                window = X[a, :, b * 16 : b * 16 + 288, :].reshape(576, C)
-                acc[...] += jnp.dot(window, kernel, preferred_element_type=jnp.float32)
+        def one(i, carry):
+            a = 1 + i * (2 * part - 1)
+            taps(s, a)
             return carry
 
         acc[...] = jnp.zeros_like(acc)
-        lax.fori_loop(0, 3, one, 0)
+        lax.fori_loop(0, 2, one, 0)
+        event6(s)
+        taps(s, 2 * (1 - part))
         for n in range(2):
             q = 2 * s + n
             base = RM[:, q].reshape(576, 128).astype(jnp.float32)
@@ -388,7 +399,7 @@
         wait_all(AX.at[0:31, m], AX.at[0:31, m], 5 + m)
 
     def send_sums():
-        grouped = to_groups([slot_sums[l] for l in range(LANES)])
+        grouped = to_groups([slot_sums[l] for l in range(LANES)], groups_of[...])
         grouped = jnp.minimum(jnp.maximum(grouped, -3e38), 3e38)
         slot_sent[...] = grouped
         slot_all[fr] = grouped
@@ -404,8 +415,8 @@
             ).start()
         )
 
-    def clip_sums():
-        wait_all(slot_all.at[0:31], slot_all.at[0:31], 8)
+    def prepare():
+        groups_of[...] = member((C, 128), 0)
         row, col = slot_vectors(slots, slot_pad)
         kind = lax.shift_right_logical(iota((8, 128), 0), 2)
         video = jnp.bitwise_and(iota((8, 128), 0), 3) * 25
@@ -418,8 +429,11 @@
         same = jnp.bitwise_and(lax.shift_right_logical(iota((8, 256), 1), 2), 1) == (
             lax.shift_right_logical(iota((8, 256), 0), 2)
         )
-        pick = jnp.where(same, pick, 0.0)
-        clip_all[y] = exact_pick(pick, slot_all[...].reshape(256, 128))
+        clip_pick[...] = jnp.where(same, pick, 0.0).astype(jnp.bfloat16)
+
+    def clip_sums():
+        wait_all(slot_all.at[0:31], slot_all.at[0:31], 8)
+        clip_all[y] = exact_pick(clip_pick[...], slot_all[...].reshape(256, 128))
         for k, peer in ((5, y_up), (6, y_dn), (7, y_op)):
             small(clip_all.at[y], clip_all.at[y], k, peer).start()
         for k, o, peer in ((5, 3, y_up), (6, 1, y_dn), (7, 2, y_op)):
@@ -473,7 +487,8 @@
             source = stats.at[wrap(y + o)]
             small(source, source, k, peer).wait_recv()
         grouped = to_groups(
-            [(stats[0, l] + stats[1, l]) + (stats[2, l] + stats[3, l]) for l in range(LANES)]
+            [(stats[0, l] + stats[1, l]) + (stats[2, l] + stats[3, l]) for l in range(LANES)],
+            groups_of[...],
         )
         grouped = grouped * (1.0 / 23040.0)
         mean = grouped[0:4]
@@ -535,6 +550,7 @@
     event1(1)
     event2(0)
     own_rows()
+    prepare()
     event1(2)
     event2(1)
     event3(0)
@@ -620,6 +636,8 @@
             pltpu.VMEM((32, 8, 128), jnp.float32),
             pltpu.VMEM((4, 8, 128), jnp.float32),
             pltpu.VMEM((1, 128), jnp.int32),
+            pltpu.VMEM((C, 128), jnp.bfloat16),
+            pltpu.VMEM((8, 256), jnp.bfloat16),
             dma((STAGES, KINDS)),
             dma((STAGES, KINDS)),
             dma((STAGES,)),
@@ -653,7 +671,9 @@
     gain,
     shift,
     bias,
+    out,
     O,
+    turned,
     W,
     H,
     RF,
@@ -716,37 +736,16 @@
     back[...] = jnp.where(pixel_t == entry_pixel(iota((512, 400), 0)), pick_t, 0.0).astype(
         jnp.bfloat16
     )
-    line = iota((112, 128), 0)
-    which = flag((frame_number(line, 2) == iota((112, 128), 1)) & (line < 100))
-    extra = jnp.dot(which, match, preferred_element_type=jnp.float32)
-    extra_pixel = entry_pixel(iota((112, 512), 1))
-    line_t = iota((128, 112), 1)
-    which_t = flag((frame_number(line_t, 2) == iota((128, 112), 0)) & (line_t < 100))
-    extra_t = jnp.dot(match_t, which_t, preferred_element_type=jnp.float32)
-    extra_pixel_t = entry_pixel(iota((512, 112), 0))
-    for i in range(4):
-        back_extra[i] = jnp.where(extra_pixel_t == i, extra_t, 0.0).astype(jnp.bfloat16)
     for n in range(5):
         both = jnp.concatenate(
             [A[:, 2 * n].reshape(512, 128), A[:, 2 * n + 1].reshape(512, 128)], axis=1
         )
         both = jnp.dot(pick, both, preferred_element_type=jnp.float32).astype(jnp.bfloat16)
         RF[:, n * 256 : n * 256 + 256] = both
-    for i in range(4):
-        picked = jnp.where(extra_pixel == i, extra, 0.0).astype(jnp.bfloat16)
-        for m in range(3):
-            if 4 * m + i < LANES:
-                l = 4 * m + i
-                RE[:, l * 128 : l * 128 + 128] = jnp.dot(
-                    picked, AX[:, m].reshape(512, 128), preferred_element_type=jnp.float32
-                ).astype(jnp.bfloat16)
-
     grouped = clip[...] * (1.0 / 576000.0)
     mean = grouped[0:4]
     rate = lax.rsqrt(grouped[4:8] - mean * mean + EPS)
     both = jnp.concatenate([rate, mean * rate], axis=0)
-    HE[0:8, :] = jnp.zeros((8, C), jnp.float32)
-    HE[104:128, :] = jnp.zeros((24, C), jnp.float32)
     H[0] = jnp.zeros((16, C), jnp.bfloat16)
     H[26] = jnp.zeros((16, C), jnp.bfloat16)
     channels = to_channels(both)
@@ -759,13 +758,6 @@
             scale_rows[o : o + 16, cols] = jnp.concatenate(
                 [jnp.broadcast_to(part[v : v + 1], (4, 128)) for v in range(4)], axis=0
             )
-        a8 = jnp.concatenate([a, a], axis=0)
-        b8 = jnp.concatenate([b, b], axis=0)
-        raw = RE[:, cols].astype(jnp.float32).reshape(14, 8, 128)
-        v = raw * a8[None] + b8[None]
-        v = (v * (1.0 / (1.0 + jnp.exp(-v)))).reshape(112, 128)
-        HE[8:108, cols] = v[0:100]
-
     def one(f, carry):
         for l in range(LANES):
             cols = slice(l * 128, l * 128 + 128)
@@ -811,9 +803,10 @@
         cols = slice(256 * n, 256 * n + 256)
         return (lambda d: OM.at[d, :, cols]), (lambda d: O.at[d, :, cols])
 
-    for n in range(5):
+    def mix(n):
         cols = slice(256 * n, 256 * n + 256)
-        loads[n].wait()
+        if n < 3:
+            loads[n].wait()
         total = RF[:, cols].astype(jnp.float32) + bias[cols].reshape(1, 256)
         for k in range(3):
             total = total + jnp.dot(
@@ -822,6 +815,41 @@
         placed = jnp.dot(back[...], total.astype(jnp.bfloat16), preferred_element_type=jnp.float32)
         OM[:, :, cols] = placed.astype(jnp.bfloat16).reshape(32, 16, 256)
         spread(*chunk(n), n)
+
+    mix(0)
+    line = iota((112, 128), 0)
+    which = flag((frame_number(line, 2) == iota((112, 128), 1)) & (line < 100))
+    extra = jnp.dot(which, match, preferred_element_type=jnp.float32)
+    extra_pixel = entry_pixel(iota((112, 512), 1))
+    line_t = iota((128, 112), 1)
+    which_t = flag((frame_number(line_t, 2) == iota((128, 112), 0)) & (line_t < 100))
+    extra_t = jnp.dot(match_t, which_t, preferred_element_type=jnp.float32)
+    extra_pixel_t = entry_pixel(iota((512, 112), 0))
+    for i in range(4):
+        back_extra[i] = jnp.where(extra_pixel_t == i, extra_t, 0.0).astype(jnp.bfloat16)
+    for i in range(4):
+        picked = jnp.where(extra_pixel == i, extra, 0.0).astype(jnp.bfloat16)
+        for m in range(3):
+            if 4 * m + i < LANES:
+                l = 4 * m + i
+                RE[:, l * 128 : l * 128 + 128] = jnp.dot(
+                    picked, AX[:, m].reshape(512, 128), preferred_element_type=jnp.float32
+                ).astype(jnp.bfloat16)
+
+    HE[0:8, :] = jnp.zeros((8, C), jnp.float32)
+    HE[104:128, :] = jnp.zeros((24, C), jnp.float32)
+    for l in range(LANES):
+        cols = slice(l * 128, l * 128 + 128)
+        a8 = jnp.concatenate([scale_rows[4 * v : 4 * v + 1, cols] for v in (0, 1, 2, 3, 0, 1, 2, 3)], axis=0)
+        b8 = jnp.concatenate([scale_rows[16 + 4 * v : 17 + 4 * v, cols] for v in (0, 1, 2, 3, 0, 1, 2, 3)], axis=0)
+        raw = RE[:, cols].astype(jnp.float32).reshape(14, 8, 128)
+        v = raw * a8[None] + b8[None]
+        v = (v * (1.0 / (1.0 + jnp.exp(-v)))).reshape(112, 128)
+        HE[8:108, cols] = v[0:100]
+    mix(1)
+    mix(2)
+    loads[3].wait()
+    loads[4].wait()
     half = pl.multiple_of(core * 640, 128)
     total = RE[:, pl.ds(half, 640)].astype(jnp.float32) + bias[pl.ds(half, 640)].reshape(1, 640)
     for k in range(3):
@@ -842,6 +870,8 @@
                 )
         OX[:, m] = placed.astype(jnp.bfloat16).reshape(32, 16, 128)
     spread((lambda d: OX.at[d]), (lambda d: BX.at[d]), 5)
+    mix(3)
+    mix(4)
     collect((lambda d: OX.at[d]), (lambda d: BX.at[d]), 5)
     for t in range(4):
         for l in range(LANES):
@@ -852,8 +882,29 @@
             O[32 + t, :, l * 128 : l * 128 + 128] = jnp.concatenate(part, axis=0).astype(
                 jnp.bfloat16
             )
+
+    def turn(n):
+        collect(*chunk(n), n)
+
+        def place(c, carry):
+            for k in range(2):
+                cols = slice(256 * n + 128 * k, 256 * n + 128 * k + 128)
+                turned[c, k, 0:16] = O[c, :, cols].astype(jnp.float32)
+                turned[c, k, 16:32] = O[c + 18, :, cols].astype(jnp.float32)
+            return carry
+
+        def fetch(c, carry):
+            for k in range(2):
+                cols = slice(256 * n + 128 * k, 256 * n + 128 * k + 128)
+                for s in range(4):
+                    out[s, c, :, cols] = turned[c, k, pl.ds(s, 8, stride=4), :].astype(jnp.bfloat16)
+            return carry
+
+        lax.fori_loop(0, 18, place, 0)
+        lax.fori_loop(0, 18, fetch, 0)
+
     for n in range(5):
-        collect(*chunk(n), n)
+        turn(n)
 
 
 def temporal_section(A, AX, clip, slots, kernel, gain, shift, bias):
@@ -862,10 +913,12 @@
     dma = pltpu.SemaphoreType.DMA
     return pl.pallas_call(
         temporal_kernel_body,
-        out_shape=jax.ShapeDtypeStruct((36, 16, C), jnp.bfloat16),
+        out_shape=jax.ShapeDtypeStruct((4, 18, 8, C), jnp.bfloat16),
         in_specs=[vmem, vmem, vmem, vmem, anywhere, vmem, vmem, vmem],
         out_specs=vmem,
         scratch_shapes=[
+            pltpu.VMEM((36, 16, C), jnp.bfloat16),
+            pltpu.VMEM((18, 2, 32, 128), jnp.float32),
             pltpu.VMEM((3, C, C), jnp.bfloat16),
             pltpu.VMEM((27, 16, C), jnp.bfloat16),
             pltpu.VMEM((400, C), jnp.bfloat16),
@@ -911,8 +964,7 @@
     tiles = temporal_section(
         main, extra, clip, frame_slot, temporal_kernel, second_gain, second_shift, temporal_bias
     )
-    result = tiles.reshape(2, 18, 4, 4, C).transpose(3, 0, 2, 1, 4)
-    return result.reshape(latents.shape)
+    return tiles.transpose(0, 2, 1, 3)
 
 
 def solution(mesh):

time: 141 us -> 136 us (0.965)
  Pallas kernels: 136 us -> 133 us
  local copies, waits for them, and re-layouts: 4.66 us -> 2.58 us
    reshape x2 -> x0, local copies, waits for them, and re-layouts: 4.09 us -> none  [the longest x1 2.79 us: body(): result = tiles.reshape(2, 18, 4, 4, C).transpose(3, 0, 2, 1, 4)]
    pallas_call x1, Pallas kernels: 107 us -> 103 us  [spatial_section(): pl.pallas_call(spatial_kernel_body, out_shape=(jax.ShapeDtypeStruct((32,...]
    unnamed x0 -> x1, local copies, waits for them, and re-layouts: none -> 2.58 us
where the time goes in v4:
time: 136 us
  Pallas kernels  133 us (98%)
  local copies, waits for them, and re-layouts  2.58 us (2%)
    pallas_call x1, Pallas kernels, spatial_section(): pl.pallas_call(spatial_kernel_body, out_shape=(jax.ShapeDtypeStruct((32,...  103 us
    pallas_call x1, Pallas kernels, temporal_section(): pl.pallas_call(temporal_kernel_body, out_shape=jax.ShapeDtypeStruct((4, 1...  30 us

profile of v4, /device:TPU:1, one launch (start us, length us, event | category | flops | bytes accessed | tf_op | source)
XLA Modules:
  0.0 135.8 jit_solution(1025627624729263367)
XLA Ops:
  0.0 103.2 %spatial.1 = (bf16[32,10,16,128]{3,2,1,0:T(8,128)(2,1)}, bf16[32,3,16,128]{3,2,1,0:T(8,128)(2,1)}, f32[8,128]{1,0:T(8,128)}) custom-call(bf16[4,18,8,1280]{3,2,1,0:T(8,128)(2,1)} %bitcast.5, f32[1280]{0:T(1024)} %gain.2, f32[1280]{0:T(1024)} %shift.2, bf16[9,40,1280]{2,1,0:T(8,128)(2,1)} %bitcast.6, f32[1280]{0:T(1024)} %bias.2, s32[1,100]{1,0:T(1,128)} %bitcast.7), custom_call_target="tpu_custom_call" | custom-call | flops 16986931200 | bytes 40000000 | tf_op jit(solution)/shard_map/spatial/pallas_call | solution.py:611
  103.2 30.0 %temporal.1 = bf16[4,18,8,1280]{3,2,1,0:T(8,128)(2,1)} custom-call(bf16[32,10,16,128]{3,2,1,0:T(8,128)(2,1)} %get-tuple-element.8.A, bf16[32,3,16,128]{3,2,1,0:T(8,128)(2,1)} %get-tuple-element.9.AX, f32[8,128]{1,0:T(8,128)} %get-tuple-element.10.clip, s32[1,100]{1,0:T(1,128)} %bitcast.8, bf16[3,1280,1280]{2,1,0:T(8,128)(2,1)} %wt.1, f32[1280]{0:T(1024)} %gain.3, ...), custom_call_target="tpu_custom_call" | custom-call | flops 4915200000 | bytes 14000000 | tf_op jit(solution)/shard_map/temporal/pallas_call | solution.py:914
  133.2 2.6 %copy.12 = bf16[4,8,18,1280]{3,1,2,0:T(8,128)(2,1)} copy(bf16[4,8,18,1280]{3,1,2,0:T(8,128)(2,1)} %bitcast.4) | data formatting | bytes 2949120

commit v5 on v4

--- a/solution.py
+++ b/solution.py
@@ -108,7 +108,6 @@
     slot_sums,
     slot_sent,
     slot_all,
-    clip_all,
     slot_pad,
     groups_of,
     clip_pick,
@@ -433,13 +432,7 @@
 
     def clip_sums():
         wait_all(slot_all.at[0:31], slot_all.at[0:31], 8)
-        clip_all[y] = exact_pick(clip_pick[...], slot_all[...].reshape(256, 128))
-        for k, peer in ((5, y_up), (6, y_dn), (7, y_op)):
-            small(clip_all.at[y], clip_all.at[y], k, peer).start()
-        for k, o, peer in ((5, 3, y_up), (6, 1, y_dn), (7, 2, y_op)):
-            source = clip_all.at[wrap(y + o)]
-            small(source, source, k, peer).wait_recv()
-        clip[...] = (clip_all[0] + clip_all[1]) + (clip_all[2] + clip_all[3])
+        clip[...] = exact_pick(clip_pick[...], slot_all[...].reshape(256, 128))
 
     def own_rows():
         lat_copy.wait()
@@ -600,8 +593,6 @@
     small(edge_out.at[1], edge_in.at[1], 1, y_dn).wait_send()
     for k, peer in ((2, y_up), (3, y_dn), (4, y_op)):
         small(stats.at[y], stats.at[y], k, peer).wait_send()
-    for k, peer in ((5, y_up), (6, y_dn), (7, y_op)):
-        small(clip_all.at[y], clip_all.at[y], k, peer).wait_send()
 
 
 def spatial_section(latents, gain, shift, kernel, bias, slots):
@@ -634,7 +625,6 @@
             pltpu.VMEM((LANES, 8, 128), jnp.float32),
             pltpu.VMEM((8, 128), jnp.float32),
             pltpu.VMEM((32, 8, 128), jnp.float32),
-            pltpu.VMEM((4, 8, 128), jnp.float32),
             pltpu.VMEM((1, 128), jnp.int32),
             pltpu.VMEM((C, 128), jnp.bfloat16),
             pltpu.VMEM((8, 256), jnp.bfloat16),
@@ -643,8 +633,8 @@
             dma((STAGES,)),
             dma((STAGES,)),
             dma((STAGES,)),
-            dma((8,)),
-            dma((8,)),
+            dma((5,)),
+            dma((5,)),
             dma,
             dma((9,)),
             dma((9,)),
@@ -686,10 +676,13 @@
     back_extra,
     scale_rows,
     slot_pad,
+    clip_all,
     w_sem,
     send,
     recv,
     own,
+    clip_send,
+    clip_recv,
 ):
     fr = lax.axis_index("frames")
     core = lax.rem(fr, 2)
@@ -703,7 +696,24 @@
     for load in loads:
         load.start()
     barrier = pltpu.get_barrier_semaphore()
+    y = lax.axis_index("rows")
+    others = [lax.rem(y + n, 4) for n in (1, 2, 3)]
+    for other in others:
+        pl.semaphore_signal(
+            barrier, inc=1, device_id={"rows": other}, device_id_type=MESH
+        )
     greet_plane(barrier, fr)
+    clip_all[y] = clip[...]
+
+    def clip_copy(n, ref):
+        return pltpu.make_async_remote_copy(
+            src_ref=ref,
+            dst_ref=ref,
+            send_sem=clip_send.at[n],
+            recv_sem=clip_recv.at[n],
+            device_id={"rows": others[n]},
+            device_id_type=MESH,
+        )
 
     row, col = slot_vectors(slots, slot_pad)
 
@@ -729,6 +739,15 @@
     pick = jnp.dot(which, match, preferred_element_type=jnp.float32)
     pixel = jnp.bitwise_and(iota((400, 512), 0), 3)
     pick = jnp.where(pixel == entry_pixel(iota((400, 512), 1)), pick, 0.0).astype(jnp.bfloat16)
+    for n in range(5):
+        both = jnp.concatenate(
+            [A[:, 2 * n].reshape(512, 128), A[:, 2 * n + 1].reshape(512, 128)], axis=1
+        )
+        both = jnp.dot(pick, both, preferred_element_type=jnp.float32).astype(jnp.bfloat16)
+        RF[:, n * 256 : n * 256 + 256] = both
+    pl.semaphore_wait(barrier, 34)
+    for n in range(3):
+        clip_copy(n, clip_all.at[y]).start()
     line_t = iota((128, 400), 1)
     which_t = flag(frame_number(line_t, 4) == iota((128, 400), 0))
     pick_t = jnp.dot(match_t, which_t, preferred_element_type=jnp.float32)
@@ -736,13 +755,9 @@
     back[...] = jnp.where(pixel_t == entry_pixel(iota((512, 400), 0)), pick_t, 0.0).astype(
         jnp.bfloat16
     )
-    for n in range(5):
-        both = jnp.concatenate(
-            [A[:, 2 * n].reshape(512, 128), A[:, 2 * n + 1].reshape(512, 128)], axis=1
-        )
-        both = jnp.dot(pick, both, preferred_element_type=jnp.float32).astype(jnp.bfloat16)
-        RF[:, n * 256 : n * 256 + 256] = both
-    grouped = clip[...] * (1.0 / 576000.0)
+    for n in range(3):
+        clip_copy(n, clip_all.at[lax.rem(y + 3 - n, 4)]).wait_recv()
+    grouped = ((clip_all[0] + clip_all[1]) + (clip_all[2] + clip_all[3])) * (1.0 / 576000.0)
     mean = grouped[0:4]
     rate = lax.rsqrt(grouped[4:8] - mean * mean + EPS)
     both = jnp.concatenate([rate, mean * rate], axis=0)
@@ -768,7 +783,6 @@
         return carry
 
     lax.fori_loop(0, 25, one, 0)
-    pl.semaphore_wait(barrier, 31)
 
     def spread(src, dst, k):
         def one(i, carry):
@@ -905,6 +919,8 @@
 
     for n in range(5):
         turn(n)
+    for n in range(3):
+        clip_copy(n, clip_all.at[y]).wait_send()
 
 
 def temporal_section(A, AX, clip, slots, kernel, gain, shift, bias):
@@ -931,10 +947,13 @@
             pltpu.VMEM((4, 512, 112), jnp.bfloat16),
             pltpu.VMEM((32, C), jnp.float32),
             pltpu.VMEM((1, 128), jnp.int32),
+            pltpu.VMEM((4, 8, 128), jnp.float32),
             dma((5,)),
             dma((6,)),
             dma((6,)),
             dma((6,)),
+            dma((3,)),
+            dma((3,)),
         ],
         compiler_params=pltpu.CompilerParams(
             collective_id=1, has_side_effects=True, vmem_limit_bytes=56 * 1024 * 1024

time: 136 us -> 136 us (level)
    pallas_call x1, Pallas kernels: 30 us -> 32.7 us  [temporal_section(): pl.pallas_call(temporal_kernel_body, out_shape=jax.ShapeDtypeStruct((4, 1...]
    pallas_call x1, Pallas kernels: 103 us -> 101 us  [spatial_section(): pl.pallas_call(spatial_kernel_body, out_shape=(jax.ShapeDtypeStruct((32,...]
where the time goes in v5:
time: 136 us
  Pallas kernels  134 us (99%)
  local copies, waits for them, and re-layouts  2.58 us (2%)
    pallas_call x1, Pallas kernels, spatial_section(): pl.pallas_call(spatial_kernel_body, out_shape=(jax.ShapeDtypeStruct((32,...  101 us
    pallas_call x1, Pallas kernels, temporal_section(): pl.pallas_call(temporal_kernel_body, out_shape=jax.ShapeDtypeStruct((4, 1...  32.7 us

profile of v5, /device:TPU:1, one launch (start us, length us, event | category | flops | bytes accessed | tf_op | source)
XLA Modules:
  0.0 136.3 jit_solution(10422244924088158570)
XLA Ops:
  0.0 101.0 %spatial.1 = (bf16[32,10,16,128]{3,2,1,0:T(8,128)(2,1)}, bf16[32,3,16,128]{3,2,1,0:T(8,128)(2,1)}, f32[8,128]{1,0:T(8,128)}) custom-call(bf16[4,18,8,1280]{3,2,1,0:T(8,128)(2,1)} %bitcast.5, f32[1280]{0:T(1024)} %gain.2, f32[1280]{0:T(1024)} %shift.2, bf16[9,40,1280]{2,1,0:T(8,128)(2,1)} %bitcast.6, f32[1280]{0:T(1024)} %bias.2, s32[1,100]{1,0:T(1,128)} %bitcast.7), custom_call_target="tpu_custom_call" | custom-call | flops 16986931200 | bytes 40000000 | tf_op jit(solution)/shard_map/spatial/pallas_call | solution.py:602
  101.0 32.7 %temporal.1 = bf16[4,18,8,1280]{3,2,1,0:T(8,128)(2,1)} custom-call(bf16[32,10,16,128]{3,2,1,0:T(8,128)(2,1)} %get-tuple-element.8.A, bf16[32,3,16,128]{3,2,1,0:T(8,128)(2,1)} %get-tuple-element.9.AX, f32[8,128]{1,0:T(8,128)} %get-tuple-element.10.clip, s32[1,100]{1,0:T(1,128)} %bitcast.8, bf16[3,1280,1280]{2,1,0:T(8,128)(2,1)} %wt.1, f32[1280]{0:T(1024)} %gain.3, ...), custom_call_target="tpu_custom_call" | custom-call | flops 4915200000 | bytes 14000000 | tf_op jit(solution)/shard_map/temporal/pallas_call | solution.py:930
  133.7 2.6 %copy.12 = bf16[4,8,18,1280]{3,1,2,0:T(8,128)(2,1)} copy(bf16[4,8,18,1280]{3,1,2,0:T(8,128)(2,1)} %bitcast.4) | data formatting | bytes 2949120

commit v6 on v4

--- a/solution.py
+++ b/solution.py
@@ -341,6 +341,11 @@
 
     def finish(s):
         span = slice(2 * s, 2 * s + 2)
+        for q in range(2 * s, 2 * s + 2):
+            value = S[:, q].astype(jnp.float32)
+            slot_sums[q] = by_slot(jnp.sum(value, axis=0), jnp.sum(value * value, axis=0))
+        if s == STAGES - 1:
+            send_sums()
         each_peer(
             lambda d: pltpu.make_async_remote_copy(
                 src_ref=S.at[d, span],
@@ -354,9 +359,6 @@
         pltpu.make_async_copy(S.at[fr, span], A.at[fr, span], a2a_own.at[s]).start()
         if s in (1, 3, 4):
             send_extra(s // 2)
-        for q in range(2 * s, 2 * s + 2):
-            value = S[:, q].astype(jnp.float32)
-            slot_sums[q] = by_slot(jnp.sum(value, axis=0), jnp.sum(value * value, axis=0))
 
     def wait_tiles(s):
         span = slice(2 * s, 2 * s + 2)
@@ -586,7 +588,6 @@
     event5(4)
     conv(4)
     finish(4)
-    send_sums()
     clip_sums()
     for s in range(STAGES):
         wait_tiles(s)

time: 136 us -> 133 us (0.978)
  Pallas kernels: 133 us -> 131 us
    pallas_call x1, Pallas kernels: 103 us -> 101 us  [spatial_section(): pl.pallas_call(spatial_kernel_body, out_shape=(jax.ShapeDtypeStruct((32,...]
where the time goes in v6:
time: 133 us
  Pallas kernels  131 us (98%)
  local copies, waits for them, and re-layouts  2.58 us (2%)
    pallas_call x1, Pallas kernels, spatial_section(): pl.pallas_call(spatial_kernel_body, out_shape=(jax.ShapeDtypeStruct((32,...  101 us
    pallas_call x1, Pallas kernels, temporal_section(): pl.pallas_call(temporal_kernel_body, out_shape=jax.ShapeDtypeStruct((4, 1...  29.8 us

profile of v6, /device:TPU:1, one launch (start us, length us, event | category | flops | bytes accessed | tf_op | source)
XLA Modules:
  0.0 133.3 jit_solution(12679326957023849921)
XLA Ops:
  0.0 100.9 %spatial.1 = (bf16[32,10,16,128]{3,2,1,0:T(8,128)(2,1)}, bf16[32,3,16,128]{3,2,1,0:T(8,128)(2,1)}, f32[8,128]{1,0:T(8,128)}) custom-call(bf16[4,18,8,1280]{3,2,1,0:T(8,128)(2,1)} %bitcast.5, f32[1280]{0:T(1024)} %gain.2, f32[1280]{0:T(1024)} %shift.2, bf16[9,40,1280]{2,1,0:T(8,128)(2,1)} %bitcast.6, f32[1280]{0:T(1024)} %bias.2, s32[1,100]{1,0:T(1,128)} %bitcast.7), custom_call_target="tpu_custom_call" | custom-call | flops 16986931200 | bytes 40000000 | tf_op jit(solution)/shard_map/spatial/pallas_call | solution.py:612
  100.9 29.8 %temporal.1 = bf16[4,18,8,1280]{3,2,1,0:T(8,128)(2,1)} custom-call(bf16[32,10,16,128]{3,2,1,0:T(8,128)(2,1)} %get-tuple-element.8.A, bf16[32,3,16,128]{3,2,1,0:T(8,128)(2,1)} %get-tuple-element.9.AX, f32[8,128]{1,0:T(8,128)} %get-tuple-element.10.clip, s32[1,100]{1,0:T(1,128)} %bitcast.8, bf16[3,1280,1280]{2,1,0:T(8,128)(2,1)} %wt.1, f32[1280]{0:T(1024)} %gain.3, ...), custom_call_target="tpu_custom_call" | custom-call | flops 4915200000 | bytes 14000000 | tf_op jit(solution)/shard_map/temporal/pallas_call | solution.py:915
  130.7 2.6 %copy.12 = bf16[4,8,18,1280]{3,1,2,0:T(8,128)(2,1)} copy(bf16[4,8,18,1280]{3,1,2,0:T(8,128)(2,1)} %bitcast.4) | data formatting | bytes 2949120
